TPU v7x, 512 devices: a whole 4x8x8 slice. The times are simulated.
512 devices in a mesh: frame: 64 (over z, y), head: 8 (over x, core).
Axes of the slice: x: 4, y: 8, z: 8, core: 2. Of those that a mesh axis runs over, the one named last changes fastest.
Arguments:
- query_space: bfloat16 [64, 512, 3072], P('frame', None, 'head'), may hold values from -48 to 48
- key_space: bfloat16 [64, 512, 3072], P('frame', None, 'head'), may hold values from -12.5 to 12.5
- value_space: bfloat16 [64, 512, 3072], P('frame', None, 'head'), may hold values from -210 to 210
- query_time: bfloat16 [64, 512, 3072], P('frame', None, 'head'), may hold values from -48 to 48
- key_time: bfloat16 [64, 512, 3072], P('frame', None, 'head'), may hold values from -12.5 to 12.5
- cotangent: bfloat16 [64, 512, 3072], P('frame', None, 'head'), may hold values from -6 to 6
- slot_clip: int32 [64], replicated, may hold values from 0 to 5, as said below
- clip_res: int32 [6], replicated, may hold values from 128 to 512, as said below
Outputs:
- mixed: bfloat16 [64, 512, 3072], P('frame', None, 'head')
- grad_query_space: bfloat16 [64, 512, 3072], P('frame', None, 'head')
- grad_key_space: bfloat16 [64, 512, 3072], P('frame', None, 'head')
- grad_value_space: bfloat16 [64, 512, 3072], P('frame', None, 'head')
- grad_query_time: bfloat16 [64, 512, 3072], P('frame', None, 'head')
- grad_key_time: bfloat16 [64, 512, 3072], P('frame', None, 'head')
Inputs may be any that keep to these rules, and one draw needn't show every extreme that they name: `slot_clip`: every clip fills two or more frame slots. `clip_res`: A multiple of 128; some clip has each bound.
All inputs are finite; a program needn't handle non-finite values.
Results may differ from a plain program's by a relative error of at most 0.012.
Values may be sent and summed in bfloat16 or wider, within the bound.
No kernel may reach another device: no remote copies, remote signals or barrier semaphores. Data moves between devices by JAX's collectives and lax.ppermute only.
A program may use at most 64 MiB of HBM per device.

v0:
```python
import jax
import jax.numpy as jnp
from jax import lax
from jax.sharding import PartitionSpec as P

HD = 128


NEGATIVE = -1e30
EPSILON = 1e-06


def attend_forward(query_rows, key_rows, value_rows, allowed, live_rows, query_label, key_label):
    score_scale = query_rows.shape[-1] ** (-0.5)
    scores = (
        jnp.einsum(
            query_label + "," + key_label + "->bhqk",
            query_rows,
            key_rows,
            preferred_element_type=jnp.float32,
        )
        * score_scale
    )
    scores = jnp.where(allowed, scores, NEGATIVE)
    highest = jnp.max(scores, axis=-1, keepdims=True)
    expanded = jnp.exp(scores - highest)
    weights = expanded / jnp.sum(expanded, axis=-1, keepdims=True)
    rounded = weights.astype(jnp.bfloat16)
    output = jnp.einsum(
        "bhqk," + key_label + "->" + query_label,
        rounded,
        value_rows,
        preferred_element_type=jnp.float32,
    )
    output = output * live_rows
    return (output, weights)


def attend_backward(query_rows, key_rows, value_rows, weights, grad_rows, query_label, key_label):
    score_scale = query_rows.shape[-1] ** (-0.5)
    rounded = weights.astype(jnp.bfloat16)
    grad_value = jnp.einsum(
        "bhqk," + query_label + "->" + key_label,
        rounded,
        grad_rows,
        preferred_element_type=jnp.float32,
    )
    grad_weights = jnp.einsum(
        query_label + "," + key_label + "->bhqk",
        grad_rows,
        value_rows,
        preferred_element_type=jnp.float32,
    )
    inner_sum = jnp.sum(weights * grad_weights, axis=-1, keepdims=True)
    grad_scores = (weights * (grad_weights - inner_sum) * score_scale).astype(jnp.bfloat16)
    grad_query = jnp.einsum(
        "bhqk," + key_label + "->" + query_label,
        grad_scores,
        key_rows,
        preferred_element_type=jnp.float32,
    )
    grad_key = jnp.einsum(
        "bhqk," + query_label + "->" + key_label,
        grad_scores,
        query_rows,
        preferred_element_type=jnp.float32,
    )
    return (grad_query, grad_key, grad_value)


def per_device(
    query_space, key_space, value_space, query_time, key_time, cotangent, slot_clip, clip_res
):
    frames_here, positions, channels = query_space.shape
    head_count = channels // HD
    full_channels = channels * lax.axis_size("head")
    positions_here = positions // lax.axis_size("frame")
    frames_total = slot_clip.shape[0]
    clip_match = slot_clip[:, None] == jnp.arange(clip_res.shape[0], dtype=jnp.int32)[None, :]
    slot_res = jnp.sum(jnp.where(clip_match, clip_res[None, :], 0), axis=1)
    local_res = lax.dynamic_slice_in_dim(
        slot_res, lax.axis_index("frame") * frames_here, frames_here, 0
    )
    live_space = jnp.arange(positions, dtype=jnp.int32)[None, :] < local_res[:, None]

    def split_heads(array):
        return array.reshape(array.shape[:-1] + (head_count, HD))

    def to_rows(array):
        return array.reshape(array.shape[0], array.shape[1], channels).astype(jnp.bfloat16)

    query_heads = split_heads(query_space)
    key_heads = split_heads(key_space)
    value_heads = split_heads(value_space)
    space_out, space_weights = attend_forward(
        query_heads,
        key_heads,
        value_heads,
        live_space[:, None, None, :],
        live_space[:, :, None, None].astype(jnp.float32),
        "bqhd",
        "bkhd",
    )
    space_flat = space_out.reshape(frames_here, positions, channels)
    square_sum = lax.psum(jnp.sum(space_flat * space_flat, axis=-1), "head")
    inverse_rms = lax.rsqrt(square_sum / full_channels + EPSILON)
    normed_full = space_flat * inverse_rms[..., None]
    normed = normed_full.astype(jnp.bfloat16)
    grad_in = jnp.where(live_space[..., None], cotangent, jnp.zeros_like(cotangent))
    here_positions = lax.axis_index("frame") * positions_here + jnp.arange(
        positions_here, dtype=jnp.int32
    )
    live_time = here_positions[None, :] < slot_res[:, None]
    same_clip = slot_clip[:, None] == slot_clip[None, :]
    diagonal = jnp.eye(frames_total, dtype=bool)
    allowed_time = same_clip[None, None] & (live_time.T[:, None, None, :] | diagonal[None, None])
    live_time_rows = live_time[:, :, None, None].astype(jnp.float32)
    query_moved, key_moved, normed_moved = (
        lax.all_to_all(query_time, "frame", split_axis=1, concat_axis=0, tiled=True),
        lax.all_to_all(key_time, "frame", split_axis=1, concat_axis=0, tiled=True),
        lax.all_to_all(normed, "frame", split_axis=1, concat_axis=0, tiled=True),
    )
    time_out, time_weights = attend_forward(
        split_heads(query_moved),
        split_heads(key_moved),
        split_heads(normed_moved),
        allowed_time,
        live_time_rows,
        "qbhd",
        "kbhd",
    )
    time_back = lax.all_to_all(to_rows(time_out), "frame", split_axis=0, concat_axis=1, tiled=True)
    grad_moved = lax.all_to_all(grad_in, "frame", split_axis=1, concat_axis=0, tiled=True)
    time_grads = attend_backward(
        split_heads(query_moved),
        split_heads(key_moved),
        split_heads(normed_moved),
        time_weights,
        split_heads(grad_moved),
        "qbhd",
        "kbhd",
    )
    grad_query_time, grad_key_time, grad_value_back = (
        lax.all_to_all(to_rows(time_grads[0]), "frame", split_axis=0, concat_axis=1, tiled=True),
        lax.all_to_all(to_rows(time_grads[1]), "frame", split_axis=0, concat_axis=1, tiled=True),
        lax.all_to_all(to_rows(time_grads[2]), "frame", split_axis=0, concat_axis=1, tiled=True),
    )
    mixed = (normed.astype(jnp.float32) + time_back.astype(jnp.float32)).astype(jnp.bfloat16)
    grad_norm = grad_in.astype(jnp.float32) + grad_value_back.astype(jnp.float32)
    inner_norm = lax.psum(jnp.sum(grad_norm * normed_full, axis=-1), "head")
    grad_space_out = (
        inverse_rms[..., None] * (grad_norm - normed_full * (inner_norm / full_channels)[..., None])
    ).astype(jnp.bfloat16)
    grad_heads = split_heads(grad_space_out)
    grad_query_space, grad_key_space, grad_value_space = attend_backward(
        query_heads, key_heads, value_heads, space_weights, grad_heads, "bqhd", "bkhd"
    )
    return (
        mixed,
        to_rows(grad_query_space),
        to_rows(grad_key_space),
        to_rows(grad_value_space),
        grad_query_time,
        grad_key_time,
    )


def solution(mesh):
    in_specs = (
        P("frame", None, "head"),
        P("frame", None, "head"),
        P("frame", None, "head"),
        P("frame", None, "head"),
        P("frame", None, "head"),
        P("frame", None, "head"),
        P(),
        P(),
    )
    out_specs = (
        P("frame", None, "head"),
        P("frame", None, "head"),
        P("frame", None, "head"),
        P("frame", None, "head"),
        P("frame", None, "head"),
        P("frame", None, "head"),
    )
    return jax.shard_map(
        per_device, mesh=mesh, in_specs=in_specs, out_specs=out_specs, check_vma=False
    )
```

profile of v0, /device:TPU:6, one launch (start us, length us, event | category | flops | bytes accessed | tf_op | source)
XLA Modules:
  0.0 229.5 jit_solution(8841201593986517372)
XLA Ops:
  0.6 0.8 select_reduce_fusion
  1.5 0.6 dynamic_slice.3
  2.0 0.6 iota_compare_fusion.2
  2.7 1.2 copy.120
  3.9 1.1 copy.121
  5.0 0.6 broadcast.248
  5.6 3.1 %reduce.9 = bf16[512,384]{1,0:T(8,128)(2,1)S(1)} reduce(bf16[512,1,384]{2,1,0:T(2,128)(2,1)S(1)} %bitcast.114, bf16[]{:T(256)} %broadcast.248), dimensions={1}, to_apply=%bitcast.89.reduce_sub_computation | reduce | bytes 786434
  8.7 0.9 reshape.529
  9.6 16.7 %all-to-all-start.4 = ((bf16[64,2,1536]{2,1,0:T(2,128)(2,1)}), bf16[64,2,1536]{2,1,0:T(2,128)(2,1)S(1)}, u32[]{:S(2)}, u32[]{:S(2)}) async-start(bf16[64,2,1536]{2,1,0:T(2,128)(2,1)} %reshape.529), calls=%async_computation.4 | async-start | bytes 786432 | tf_op jit(solution)/shard_map/all_to_all | solution.py:133
  26.3 0.6 copy.185
  27.0 3.0 %reduce.11 = bf16[512,384]{1,0:T(8,128)(2,1)S(1)} reduce(bf16[512,1,384]{2,1,0:T(2,128)(2,1)S(1)} %bitcast.118, bf16[]{:T(256)} %broadcast.248), dimensions={1}, to_apply=%bitcast.113.reduce_sub_computation | reduce | bytes 786434
  30.0 0.9 reshape.527
  30.9 12.8 %all-to-all-done.4 = bf16[64,2,1536]{2,1,0:T(2,128)(2,1)S(1)} async-done(((bf16[64,2,1536]{2,1,0:T(2,128)(2,1)}), bf16[64,2,1536]{2,1,0:T(2,128)(2,1)S(1)}, u32[]{:S(2)}, u32[]{:S(2)}) %all-to-all-start.4) | async-done | bytes 393248 | tf_op jit(solution)/shard_map/all_to_all | solution.py:133
  43.7 4.8 %all-to-all-start.1 = ((bf16[64,2,1536]{2,1,0:T(2,128)(2,1)}), bf16[64,2,1536]{2,1,0:T(2,128)(2,1)S(1)}, u32[]{:S(2)}, u32[]{:S(2)}) async-start(bf16[64,2,1536]{2,1,0:T(2,128)(2,1)} %reshape.527), calls=%async_computation.1 | async-start | bytes 786432 | tf_op jit(solution)/shard_map/all_to_all | solution.py:119
  48.5 0.9 copy.102
  49.6 0.6 copy.184
  50.3 3.0 %reduce.10 = bf16[512,384]{1,0:T(8,128)(2,1)S(1)} reduce(bf16[512,1,384]{2,1,0:T(2,128)(2,1)S(1)} %bitcast.119, bf16[]{:T(256)} %broadcast.248), dimensions={1}, to_apply=%bitcast.112.reduce_sub_computation | reduce | bytes 786434
  53.3 0.9 reshape.525
  54.2 10.5 %all-to-all-done.1 = bf16[64,2,1536]{2,1,0:T(2,128)(2,1)S(1)} async-done(((bf16[64,2,1536]{2,1,0:T(2,128)(2,1)}), bf16[64,2,1536]{2,1,0:T(2,128)(2,1)S(1)}, u32[]{:S(2)}, u32[]{:S(2)}) %all-to-all-start.1) | async-done | bytes 393248 | tf_op jit(solution)/shard_map/all_to_all | solution.py:119
  64.7 4.6 %all-to-all-start.2 = ((bf16[64,2,1536]{2,1,0:T(2,128)(2,1)}), bf16[64,2,1536]{2,1,0:T(2,128)(2,1)S(1)}, u32[]{:S(2)}, u32[]{:S(2)}) async-start(bf16[64,2,1536]{2,1,0:T(2,128)(2,1)} %reshape.525), calls=%async_computation.2 | async-start | bytes 786432 | tf_op jit(solution)/shard_map/all_to_all | solution.py:120
  69.5 0.8 or_and_fusion
  70.3 0.3 reshape.530
  70.7 0.3 reshape.528
  71.0 14.7 %all-to-all-done.2 = bf16[64,2,1536]{2,1,0:T(2,128)(2,1)S(1)} async-done(((bf16[64,2,1536]{2,1,0:T(2,128)(2,1)}), bf16[64,2,1536]{2,1,0:T(2,128)(2,1)S(1)}, u32[]{:S(2)}, u32[]{:S(2)}) %all-to-all-start.2) | async-done | bytes 393248 | tf_op jit(solution)/shard_map/all_to_all | solution.py:120
  85.7 0.3 reshape.526
  86.2 0.7 copy-done.4
  86.9 1.2 fusion.23
  88.1 1.1 fusion.73
  89.3 0.3 fusion.37
  89.6 1.0 copy.180
  90.6 4.8 %all-to-all-start.5 = ((bf16[64,8,384]{2,1,0:T(8,128)(2,1)}), bf16[64,8,384]{2,1,0:T(8,128)(2,1)S(1)}, u32[]{:S(2)}, u32[]{:S(2)}) async-start(bf16[64,8,384]{2,1,0:T(8,128)(2,1)} %bitcast.108), calls=%async_computation.5 | async-start | bytes 786432 | tf_op jit(solution)/shard_map/all_to_all | solution.py:146
  95.4 3.0 %fusion.72 = (f32[3,512]{1,0:T(4,128)S(1)}, f32[3,512,512]{1,2,0:T(8,128)}) fusion(pred[512]{0:T(512)(128)(4,1)S(1)} %get-tuple-element.38, bf16[512,3,128]{0,2,1:T(8,128)(2,1)S(1)} %bitcast.134, bf16[512,3,128]{0,2,1:T(8,128)(2,1)S(1)} %bitcast.132), kind=kOutput, calls=%fused_computation.101 | convolution fusion | flops 204472832 | bytes 3938816 | tf_op jit(solution)/shard_map/sub | solution.py:26
  98.6 2.5 %fusion.42 = (f32[512]{0:T(512)S(1)}, f32[1,3,128,512]{3,2,1,0:T(8,128)S(1)}) fusion(f32[512]{0:T(512)S(1)} %get-tuple-element.39, bf16[512,3,128]{0,2,1:T(8,128)(2,1)S(1)} %bitcast.130, f32[3,512,512]{1,2,0:T(8,128)} %get-tuple-element.33, f32[3,512]{1,0:T(4,128)S(1)} %get-tuple-element.32), kind=kOutput, calls=%fused_computation.45 | convolution fusion | flops 203488768 | bytes 4335616 | tf_op jit(solution)/shard_map/bhqk,bkhd->bqhd/dot_general | solution.py:29
  101.1 10.6 %psum.14 = f32[1,512]{1,0:T(1,128)S(1)} all-reduce(f32[1,512]{1,0:T(1,128)S(1)} %bitcast.143), channel_id=1, replica_groups=mesh['frame'=64,'head'=8] {'head'}, use_global_device_ids=true, to_apply=%region_4.5 | all-reduce | flops 512 | bytes 4096 | tf_op jit(solution)/shard_map/psum | solution.py:105
  111.7 0.3 copy.125
  112.2 12.3 %psum.15 = f32[1,512]{1,0:T(1,128)S(1)} all-reduce(f32[1,512]{1,0:T(1,128)S(1)} %bitcast.142), channel_id=1, replica_groups=mesh['frame'=64,'head'=8] {'head'}, use_global_device_ids=true, to_apply=%region_8.9 | all-reduce | flops 512 | bytes 4096 | tf_op jit(solution)/shard_map/psum | solution.py:150
  124.5 1.0 multiply_convert_fusion.1
  125.5 1.1 copy.108
  126.6 3.1 %reduce.12 = bf16[512,384]{1,0:T(8,128)(2,1)S(1)} reduce(bf16[512,1,384]{2,1,0:T(2,128)(2,1)S(1)} %bitcast.116, bf16[]{:T(256)} %broadcast.248), dimensions={1}, to_apply=%bitcast.83.reduce_sub_computation | reduce | bytes 786434
  129.8 29.0 %all_to_all.38 = bf16[64,2,1536]{2,1,0:T(2,128)(2,1)S(1)} all-to-all(bf16[64,2,1536]{2,1,0:T(2,128)(2,1)S(1)} %reshape.523), channel_id=1, replica_groups=mesh['frame'=64,'head'=8] {'frame'}, dimensions={0} | all-to-all | bytes 786432 | tf_op jit(solution)/shard_map/all_to_all | solution.py:121
  158.9 0.3 reshape.524
  159.3 0.3 fusion.48
  159.6 1.9 fusion.35
  161.5 1.0 copy.179
  162.5 5.2 %all-to-all-start.6 = ((bf16[64,8,384]{2,1,0:T(8,128)(2,1)}), bf16[64,8,384]{2,1,0:T(8,128)(2,1)S(1)}, u32[]{:S(2)}, u32[]{:S(2)}) async-start(bf16[64,8,384]{2,1,0:T(8,128)(2,1)} %bitcast.107), calls=%async_computation.6 | async-start | bytes 786432 | tf_op jit(solution)/shard_map/all_to_all | solution.py:144
  167.7 1.8 fusion.36
  169.6 1.0 copy.178
  170.6 14.0 %all-to-all-done.6 = bf16[64,8,384]{2,1,0:T(8,128)(2,1)S(1)} async-done(((bf16[64,8,384]{2,1,0:T(8,128)(2,1)}), bf16[64,8,384]{2,1,0:T(8,128)(2,1)S(1)}, u32[]{:S(2)}, u32[]{:S(2)}) %all-to-all-start.6) | async-done | bytes 393248 | tf_op jit(solution)/shard_map/all_to_all | solution.py:144
  184.6 4.6 %all-to-all-start.7 = ((bf16[64,8,384]{2,1,0:T(8,128)(2,1)}), bf16[64,8,384]{2,1,0:T(8,128)(2,1)S(1)}, u32[]{:S(2)}, u32[]{:S(2)}) async-start(bf16[64,8,384]{2,1,0:T(8,128)(2,1)} %bitcast.106), calls=%async_computation.7 | async-start | bytes 786432 | tf_op jit(solution)/shard_map/all_to_all | solution.py:145
  189.3 2.5 %convolution_convert_fusion = bf16[3,128,512]{2,1,0:T(8,128)(2,1)S(1)} fusion(bf16[512,3,128]{0,2,1:T(8,128)(2,1)S(1)} %bitcast.128, f32[3,512,512]{1,2,0:T(8,128)} %get-tuple-element.33, f32[3,512]{1,0:T(4,128)S(1)} %copy-done.21), kind=kOutput, calls=%fused_computation.33 | convolution fusion | flops 203096064 | bytes 3938304 | tf_op jit(solution)/shard_map/bhqk,bqhd->bkhd/dot_general | solution.py:42
  191.8 0.9 copy.141
  192.8 1.8 fusion.28
  194.5 1.0 copy.182
  195.5 9.9 %all-to-all-done.7 = bf16[64,8,384]{2,1,0:T(8,128)(2,1)S(1)} async-done(((bf16[64,8,384]{2,1,0:T(8,128)(2,1)}), bf16[64,8,384]{2,1,0:T(8,128)(2,1)S(1)}, u32[]{:S(2)}, u32[]{:S(2)}) %all-to-all-start.7) | async-done | bytes 393248 | tf_op jit(solution)/shard_map/all_to_all | solution.py:145
  205.5 4.9 %all-to-all-start.3 = ((bf16[64,8,384]{2,1,0:T(8,128)(2,1)}), bf16[64,8,384]{2,1,0:T(8,128)(2,1)S(1)}, u32[]{:S(2)}, u32[]{:S(2)}) async-start(bf16[64,8,384]{2,1,0:T(8,128)(2,1)} %bitcast.110), calls=%async_computation.3 | async-start | bytes 786432 | tf_op jit(solution)/shard_map/all_to_all | solution.py:132
  210.4 2.3 %fusion.74 = f32[3,512,512]{1,2,0:T(8,128)} fusion(bf16[512,3,128]{0,2,1:T(8,128)(2,1)S(1)} %bitcast.129, bf16[512,3,128]{0,2,1:T(8,128)(2,1)S(1)} %bitcast.131), kind=kOutput, calls=%fused_computation.105 | convolution fusion | flops 201326592 | bytes 3932160 | tf_op jit(solution)/shard_map/bqhd,bkhd->bhqk/dot_general | solution.py:48
  212.7 6.0 %fusion.32 = bf16[3,512,128]{1,2,0:T(8,128)(2,1)S(1)} fusion(bf16[512,3,128]{0,2,1:T(8,128)(2,1)S(1)} %bitcast.135, f32[3,512,512]{1,2,0:T(8,128)} %fusion.74, f32[3,512,512]{1,2,0:T(8,128)} %get-tuple-element.33, f32[3,512]{1,0:T(4,128)S(1)} %copy-done.21), kind=kOutput, calls=%fused_computation.32 | convolution fusion | flops 207030272 | bytes 7084032 | tf_op jit(solution)/shard_map/bhqk,bqhd->bkhd/dot_general | solution.py:62
  218.7 0.9 copy.140
  219.6 6.1 %fusion.29 = bf16[3,512,128]{1,2,0:T(8,128)(2,1)S(1)} fusion(bf16[512,3,128]{0,2,1:T(8,128)(2,1)S(1)} %bitcast.133, f32[3,512,512]{1,2,0:T(8,128)} %fusion.74, f32[3,512,512]{1,2,0:T(8,128)} %get-tuple-element.33, f32[3,512]{1,0:T(4,128)S(1)} %copy-done.21), kind=kOutput, calls=%fused_computation.31 | convolution fusion | flops 207030272 | bytes 7084032 | tf_op jit(solution)/shard_map/bhqk,bkhd->bqhd/dot_general | solution.py:56
  225.7 0.9 copy.139
  226.7 0.3 copy.119
  227.1 0.9 copy.138
  228.0 0.7 copy.188
  228.7 0.7 copy.189
  (62 shorter events, 1.6 us)
Async XLA Ops:
  0.6 25.7 %copy-start.15 = (bf16[1,512,384]{2,1,0:T(8,128)(2,1)S(1)}, bf16[1,512,384]{2,1,0:T(8,128)(2,1)}, u32[]{:S(2)}) copy-start(bf16[1,512,384]{2,1,0:T(8,128)(2,1)} %param.11) | copy-start | bytes 1179652
  5.6 42.9 %copy-start.8 = (bf16[1,512,384]{2,1,0:T(8,128)(2,1)S(1)}, bf16[1,512,384]{2,1,0:T(8,128)(2,1)}, u32[]{:S(2)}) copy-start(bf16[1,512,384]{2,1,0:T(8,128)(2,1)} %param.8) | copy-start | bytes 1179652
  8.7 40.7 %copy-start.9 = (bf16[1,512,384]{2,1,0:T(8,128)(2,1)S(1)}, bf16[1,512,384]{2,1,0:T(8,128)(2,1)}, u32[]{:S(2)}) copy-start(bf16[1,512,384]{2,1,0:T(8,128)(2,1)} %param.9) | copy-start | bytes 1179652
  9.6 40.0 %copy-start.16 = (bf16[1,512,384]{2,1,0:T(8,128)(2,1)S(1)}, bf16[1,512,384]{2,1,0:T(8,128)(2,1)}, u32[]{:S(2)}) copy-start(bf16[1,512,384]{2,1,0:T(8,128)(2,1)} %param.12) | copy-start | bytes 1179652
  9.6 34.1 %all-to-all-start.4 = ((bf16[64,2,1536]{2,1,0:T(2,128)(2,1)}), bf16[64,2,1536]{2,1,0:T(2,128)(2,1)S(1)}, u32[]{:S(2)}, u32[]{:S(2)}) async-start(bf16[64,2,1536]{2,1,0:T(2,128)(2,1)} %reshape.529), calls=%async_computation.4 | async-start | bytes 786432 | tf_op jit(solution)/shard_map/all_to_all | solution.py:133
  30.9 38.5 %copy-start.19 = (s32[64]{0:T(128)S(1)}, s32[64]{0:T(128)}, u32[]{:S(2)}) copy-start(s32[64]{0:T(128)} %param.14) | copy-start | bytes 772
  43.7 21.1 %all-to-all-start.1 = ((bf16[64,2,1536]{2,1,0:T(2,128)(2,1)}), bf16[64,2,1536]{2,1,0:T(2,128)(2,1)S(1)}, u32[]{:S(2)}, u32[]{:S(2)}) async-start(bf16[64,2,1536]{2,1,0:T(2,128)(2,1)} %reshape.527), calls=%async_computation.1 | async-start | bytes 786432 | tf_op jit(solution)/shard_map/all_to_all | solution.py:119
  49.6 45.7 %copy-start.11 = (bf16[1,512,384]{1,2,0:T(8,128)(2,1)}, bf16[1,512,384]{1,2,0:T(8,128)(2,1)S(1)}, u32[]{:S(2)}) copy-start(bf16[1,512,384]{1,2,0:T(8,128)(2,1)S(1)} %copy.103) | copy-start | bytes 1179652
  64.7 21.0 %all-to-all-start.2 = ((bf16[64,2,1536]{2,1,0:T(2,128)(2,1)}), bf16[64,2,1536]{2,1,0:T(2,128)(2,1)S(1)}, u32[]{:S(2)}, u32[]{:S(2)}) async-start(bf16[64,2,1536]{2,1,0:T(2,128)(2,1)} %reshape.525), calls=%async_computation.2 | async-start | bytes 786432 | tf_op jit(solution)/shard_map/all_to_all | solution.py:120
  86.2 0.7 copy-start.4
  86.2 1.9 copy-start.6
  88.1 2.5 %copy-start.3 = (f32[8,3,64,64]{2,3,1,0:T(8,128)}, f32[8,3,64,64]{2,3,1,0:T(8,128)S(1)}, u32[]{:S(2)}) copy-start(f32[8,3,64,64]{2,3,1,0:T(8,128)S(1)} %fusion.23) | copy-start | bytes 1179652
  89.2 9.1 %copy-start.17 = (f32[8,3,64]{2,1,0:T(4,128)}, f32[8,3,64]{2,1,0:T(4,128)S(1)}, u32[]{:S(2)}) copy-start(f32[8,3,64]{2,1,0:T(4,128)S(1)} %get-tuple-element.34) | copy-start | bytes 18436
  89.2 6.1 %copy-start.13 = (bf16[1,512,384]{1,2,0:T(8,128)(2,1)S(1)}, bf16[1,512,384]{1,2,0:T(8,128)(2,1)}, u32[]{:S(2)}) copy-start(bf16[1,512,384]{1,2,0:T(8,128)(2,1)} %copy.102) | copy-start | bytes 1179652
  90.6 7.8 %copy-start.10 = (bf16[1,512,384]{2,1,0:T(8,128)(2,1)S(1)}, bf16[1,512,384]{2,1,0:T(8,128)(2,1)}, u32[]{:S(2)}) copy-start(bf16[1,512,384]{2,1,0:T(8,128)(2,1)} %param.10) | copy-start | bytes 1179652
  90.6 21.1 %all-to-all-start.5 = ((bf16[64,8,384]{2,1,0:T(8,128)(2,1)}), bf16[64,8,384]{2,1,0:T(8,128)(2,1)S(1)}, u32[]{:S(2)}, u32[]{:S(2)}) async-start(bf16[64,8,384]{2,1,0:T(8,128)(2,1)} %bitcast.108), calls=%async_computation.5 | async-start | bytes 786432 | tf_op jit(solution)/shard_map/all_to_all | solution.py:146
  98.4 2.7 %copy-start.20 = (f32[3,512]{1,0:T(4,128)}, f32[3,512]{1,0:T(4,128)S(1)}, u32[]{:S(2)}) copy-start(f32[3,512]{1,0:T(4,128)S(1)} %get-tuple-element.32) | copy-start | bytes 18436
  98.6 2.5 %copy-start.1 = (bf16[1,512,384]{1,2,0:T(8,128)(2,1)}, bf16[1,512,384]{1,2,0:T(8,128)(2,1)S(1)}, u32[]{:S(2)}) copy-start(bf16[1,512,384]{1,2,0:T(8,128)(2,1)S(1)} %copy.106) | copy-start | bytes 1179652
  126.6 33.1 %copy-start.7 = (bf16[64,8,3,128]{3,1,2,0:T(8,128)(2,1)S(1)}, bf16[64,8,3,128]{3,1,2,0:T(8,128)(2,1)}, u32[]{:S(2)}) copy-start(bf16[64,8,3,128]{3,1,2,0:T(8,128)(2,1)} %copy-done.6) | copy-start | bytes 1179652
  126.6 33.1 %copy-start.18 = (f32[8,3,64]{2,1,0:T(4,128)S(1)}, f32[8,3,64]{2,1,0:T(4,128)}, u32[]{:S(2)}) copy-start(f32[8,3,64]{2,1,0:T(4,128)} %copy-done.17) | copy-start | bytes 18436
  159.6 8.1 %copy-start.5 = (bf16[64,8,3,128]{3,1,2,0:T(8,128)(2,1)S(1)}, bf16[64,8,3,128]{3,1,2,0:T(8,128)(2,1)}, u32[]{:S(2)}) copy-start(bf16[64,8,3,128]{3,1,2,0:T(8,128)(2,1)} %copy-done.4) | copy-start | bytes 1179652
  162.5 22.1 %all-to-all-start.6 = ((bf16[64,8,384]{2,1,0:T(8,128)(2,1)}), bf16[64,8,384]{2,1,0:T(8,128)(2,1)S(1)}, u32[]{:S(2)}, u32[]{:S(2)}) async-start(bf16[64,8,384]{2,1,0:T(8,128)(2,1)} %bitcast.107), calls=%async_computation.6 | async-start | bytes 786432 | tf_op jit(solution)/shard_map/all_to_all | solution.py:144
  167.7 21.6 %copy-start = (bf16[1,512,384]{1,2,0:T(8,128)(2,1)S(1)}, bf16[1,512,384]{1,2,0:T(8,128)(2,1)}, u32[]{:S(2)}) copy-start(bf16[1,512,384]{1,2,0:T(8,128)(2,1)} %get-tuple-element.30) | copy-start | bytes 1179652
  167.7 21.6 %copy-start.21 = (f32[3,512]{1,0:T(4,128)S(1)}, f32[3,512]{1,0:T(4,128)}, u32[]{:S(2)}) copy-start(f32[3,512]{1,0:T(4,128)} %copy-done.20) | copy-start | bytes 18436
  184.6 20.9 %all-to-all-start.7 = ((bf16[64,8,384]{2,1,0:T(8,128)(2,1)}), bf16[64,8,384]{2,1,0:T(8,128)(2,1)S(1)}, u32[]{:S(2)}, u32[]{:S(2)}) async-start(bf16[64,8,384]{2,1,0:T(8,128)(2,1)} %bitcast.106), calls=%async_computation.7 | async-start | bytes 786432 | tf_op jit(solution)/shard_map/all_to_all | solution.py:145
  191.8 18.5 %copy-start.2 = (bf16[1,512,384]{1,2,0:T(8,128)(2,1)S(1)}, bf16[1,512,384]{1,2,0:T(8,128)(2,1)}, u32[]{:S(2)}) copy-start(bf16[1,512,384]{1,2,0:T(8,128)(2,1)} %copy-done.1) | copy-start | bytes 1179652
  194.5 18.2 %copy-start.14 = (bf16[1,512,384]{1,2,0:T(8,128)(2,1)S(1)}, bf16[1,512,384]{1,2,0:T(8,128)(2,1)}, u32[]{:S(2)}) copy-start(bf16[1,512,384]{1,2,0:T(8,128)(2,1)} %copy.102) | copy-start | bytes 1179652
  205.5 21.2 %all-to-all-start.3 = ((bf16[64,8,384]{2,1,0:T(8,128)(2,1)}), bf16[64,8,384]{2,1,0:T(8,128)(2,1)S(1)}, u32[]{:S(2)}, u32[]{:S(2)}) async-start(bf16[64,8,384]{2,1,0:T(8,128)(2,1)} %bitcast.110), calls=%async_computation.3 | async-start | bytes 786432 | tf_op jit(solution)/shard_map/all_to_all | solution.py:132
  212.7 6.9 %copy-start.12 = (bf16[1,512,384]{1,2,0:T(8,128)(2,1)S(1)}, bf16[1,512,384]{1,2,0:T(8,128)(2,1)}, u32[]{:S(2)}) copy-start(bf16[1,512,384]{1,2,0:T(8,128)(2,1)} %copy-done.11) | copy-start | bytes 1179652
where the time goes:
time: 232 us; the launch traced here: 229 us
  waiting for transfers between devices  61.8 us (27%)
  blocking collectives  51.9 us (22%)
  starting transfers between devices  45.6 us (20%)
  matrix products  29.6 us (13%)
  local copies, waits for them, and re-layouts  22 us (9%)
  other arithmetic  17.3 us (7%)
    all_to_all x1, blocking collectives, per_device(): lax.all_to_all(normed, 'frame', split_axis=1, concat_axis=0, tiled=True)  29 us
    all_to_all x1, starting transfers between devices, per_device(): lax.all_to_all(grad_in, 'frame', split_axis=1, concat_axis=0, tiled=True)  16.7 us
    all_to_all x1, waiting for transfers between devices, per_device(): lax.all_to_all(key_time, 'frame', split_axis=1, concat_axis=0, tiled=True)  14.7 us
    unnamed x65, local copies, waits for them, and re-layouts  14.4 us
    all_to_all x1, waiting for transfers between devices, per_device(): lax.all_to_all(to_rows(time_grads[0]), 'frame', split_axis=0, concat_axis...  14 us
    all_to_all x1, waiting for transfers between devices, per_device(): lax.all_to_all(grad_in, 'frame', split_axis=1, concat_axis=0, tiled=True)  12.8 us
    unnamed x4, other arithmetic  12.3 us
    psum x1, blocking collectives, per_device(): inner_norm = lax.psum(jnp.sum(grad_norm * normed_full, axis=-1), 'head')  12.3 us
  transfers between devices with their start and end apart: 7, of which 5 were waited for; matrix products, arithmetic and copies ran while one was open for 19% of the time, Pallas kernels for 0%

commit v1 on v0

v1 whole, which is shorter than its diff:
```python
import jax
import jax.numpy as jnp
from jax import lax
from jax.experimental import pallas as pl
from jax.experimental.pallas import tpu as pltpu
from jax.sharding import PartitionSpec as P

HD = 128
NEGATIVE = -1e30
EPSILON = 1e-06
LOG2E = 1.4426950408889634
F32 = jnp.float32
BF16 = jnp.bfloat16
VMEM_BYTES = 32 * 1024 * 1024


def dot(a, b, ca, cb):
    return lax.dot_general(a, b, (((ca,), (cb,)), ((), ())), preferred_element_type=F32)


def softmax_keys_first(q, k, q_mask, k_mask):
    scale = HD ** (-0.5)
    scores = dot(
        jnp.concatenate([k, k_mask], axis=1), jnp.concatenate([q, q_mask], axis=1), 1, 1
    )
    highest = jnp.max(scores, axis=0, keepdims=True)
    expanded = jnp.exp2((scores - highest) * (scale * LOG2E))
    return expanded, 1.0 / jnp.sum(expanded, axis=0, keepdims=True)


def softmax_queries_first(q, k, q_mask, k_mask):
    scale = HD ** (-0.5)
    scores = dot(
        jnp.concatenate([q, q_mask], axis=1), jnp.concatenate([k, k_mask], axis=1), 1, 1
    )
    highest = jnp.max(scores, axis=1, keepdims=True)
    expanded = jnp.exp2((scores - highest) * (scale * LOG2E))
    return expanded, 1.0 / jnp.sum(expanded, axis=1, keepdims=True)


def pack_kernel(a_ref, b_ref, c_ref, out_ref):
    out_ref[:, :HD] = a_ref[...]
    out_ref[:, HD : 2 * HD] = b_ref[...]
    out_ref[:, 2 * HD :] = c_ref[...]


def space_forward_kernel(q_ref, k_ref, v_ref, q_mask_ref, k_mask_ref, live_ref, out_ref):
    expanded, inverse = softmax_queries_first(
        q_ref[...], k_ref[...], q_mask_ref[...], k_mask_ref[...]
    )
    weights = (expanded * inverse).astype(BF16)
    out_ref[...] = dot(weights, v_ref[...], 1, 0) * live_ref[...]


def space_backward_kernel(
    q_ref, k_ref, v_ref, g_ref, q_mask_ref, k_mask_ref, gq_ref, gk_ref, gv_ref
):
    scale = HD ** (-0.5)
    q, k, v, g = q_ref[...], k_ref[...], v_ref[...], g_ref[...]
    expanded, inverse = softmax_keys_first(q, k, q_mask_ref[...], k_mask_ref[...])
    weights = expanded * inverse
    gv_ref[...] = dot(weights.astype(BF16), g, 1, 0).astype(BF16)
    grad_weights = dot(v, g, 1, 1)
    inner = jnp.sum(weights * grad_weights, axis=0, keepdims=True)
    grad_scores = (weights * (grad_weights - inner) * scale).astype(BF16)
    gk_ref[...] = dot(grad_scores, q, 1, 0).astype(BF16)
    gq_ref[...] = dot(grad_scores, k, 0, 0).astype(BF16)


def time_value_kernel(moved_ref, normed_ref, q_mask_ref, k_mask_ref, live_ref, out_ref):
    q, k, g = moved_ref[:, :HD], moved_ref[:, HD : 2 * HD], moved_ref[:, 2 * HD :]
    expanded, inverse = softmax_keys_first(q, k, q_mask_ref[...], k_mask_ref[...])
    weights = (expanded * (inverse * live_ref[...])).astype(BF16)
    out_ref[:, :HD] = normed_ref[...]
    out_ref[:, HD:] = dot(weights, g, 1, 0).astype(BF16)


def time_weights_kernel(moved_ref, q_mask_ref, k_mask_ref, live_ref, weights_ref):
    q, k = moved_ref[:, :HD], moved_ref[:, HD : 2 * HD]
    expanded, inverse = softmax_keys_first(q, k, q_mask_ref[...], k_mask_ref[...])
    weights_ref[0] = expanded * (inverse * live_ref[...])


def time_rest_kernel(moved_ref, normed_ref, weights_ref, out_ref):
    scale = HD ** (-0.5)
    q, k, g = moved_ref[:, :HD], moved_ref[:, HD : 2 * HD], moved_ref[:, 2 * HD :]
    v = normed_ref[...]
    weights = weights_ref[0]
    out_ref[:, :HD] = dot(weights.astype(BF16), v, 0, 0).astype(BF16)
    grad_weights = dot(v, g, 1, 1)
    inner = jnp.sum(weights * grad_weights, axis=0, keepdims=True)
    grad_scores = (weights * (grad_weights - inner) * scale).astype(BF16)
    out_ref[:, HD : 2 * HD] = dot(grad_scores, k, 0, 0).astype(BF16)
    out_ref[:, 2 * HD :] = dot(grad_scores, q, 1, 0).astype(BF16)


def finish_kernel(back_ref, normed_ref, mixed_ref, gq_ref, gk_ref):
    mixed_ref[...] = (
        normed_ref[...].astype(F32) + back_ref[:, :HD].astype(F32)
    ).astype(BF16)
    gq_ref[...] = back_ref[:, HD : 2 * HD]
    gk_ref[...] = back_ref[:, 2 * HD :]


def per_device(
    query_space, key_space, value_space, query_time, key_time, cotangent, slot_clip, clip_res
):
    _, rows, channels = query_space.shape
    head_count = channels // HD
    frames = slot_clip.shape[0]
    full_channels = channels * lax.axis_size("head")
    positions_here = rows // lax.axis_size("frame")
    here = lax.axis_index("frame")

    def head_block(width=1):
        return pl.BlockSpec((rows, width * HD), lambda h: (0, h))

    def shared(shape):
        return pl.BlockSpec(shape, lambda h: (0,) * len(shape))

    def call(kernel, in_specs, out_specs, out_shape, flops=0, traffic=0):
        return pl.pallas_call(
            kernel,
            grid=(head_count,),
            in_specs=in_specs,
            out_specs=out_specs,
            out_shape=out_shape,
            compiler_params=pltpu.CompilerParams(
                dimension_semantics=("arbitrary",), vmem_limit_bytes=VMEM_BYTES
            ),
            cost_estimate=pl.CostEstimate(
                flops=flops, bytes_accessed=traffic, transcendentals=0
            ),
        )

    def exchange(array):
        width = array.shape[-1]
        blocks = array.reshape(frames, positions_here, width)
        moved = lax.all_to_all(blocks, "frame", split_axis=0, concat_axis=0, tiled=True)
        return moved.reshape(rows, width)

    whole = jax.ShapeDtypeStruct((rows, channels), BF16)
    product = 2 * rows * rows * HD * head_count
    size = rows * channels * 2

    q_space, k_space, v_space = query_space[0], key_space[0], value_space[0]

    packed = call(
        pack_kernel,
        [head_block()] * 3,
        head_block(3),
        jax.ShapeDtypeStruct((rows, 3 * channels), BF16),
        traffic=6 * size,
    )(query_time[0], key_time[0], cotangent[0])
    moved = exchange(packed)

    clip_match = slot_clip[:, None] == jnp.arange(clip_res.shape[0], dtype=jnp.int32)[None, :]
    slot_res = jnp.sum(jnp.where(clip_match, clip_res[None, :], 0), axis=1)
    local_res = lax.dynamic_slice_in_dim(slot_res, here, 1, 0)
    live_space = jnp.arange(rows, dtype=jnp.int32) < local_res
    column = jnp.arange(HD, dtype=jnp.int32)[None, :]
    space_q_mask = jnp.broadcast_to(column == 0, (rows, HD)).astype(BF16)
    space_k_mask = jnp.where(live_space[:, None], 0.0, NEGATIVE).astype(BF16)
    space_k_mask = jnp.broadcast_to(space_k_mask, (rows, HD))
    place = jnp.arange(positions_here, dtype=jnp.int32)[None, :]
    live_time = (here * positions_here + place) < slot_res[:, None]
    group = slot_clip[:, None] * positions_here + place
    group = group.reshape(rows, 1)
    time_q_mask = (column == group).astype(BF16)
    time_k_mask = jnp.where((column == group) & live_time.reshape(rows, 1), 0.0, NEGATIVE)
    time_k_mask = time_k_mask.astype(BF16)
    live_row = live_time.reshape(1, rows).astype(F32)

    mask_spec = shared((rows, HD))
    space_out = call(
        space_forward_kernel,
        [head_block()] * 3 + [mask_spec, mask_spec, shared((rows, 1))],
        head_block(),
        jax.ShapeDtypeStruct((rows, channels), F32),
        flops=3 * product,
        traffic=5 * size,
    )(q_space, k_space, v_space, space_q_mask, space_k_mask, live_space[:, None].astype(F32))
    square_sum = lax.psum(jnp.sum(space_out * space_out, axis=-1), "head")
    inverse_rms = lax.rsqrt(square_sum / full_channels + EPSILON)
    normed_full = space_out * inverse_rms[:, None]
    normed = normed_full.astype(BF16)

    pair = call(
        time_value_kernel,
        [head_block(3), head_block(), mask_spec, mask_spec, shared((1, rows))],
        head_block(2),
        jax.ShapeDtypeStruct((rows, 2 * channels), BF16),
        flops=3 * product,
        traffic=6 * size,
    )(moved, normed, time_q_mask, time_k_mask, live_row)
    pair_moved = exchange(pair)
    weights_spec = pl.BlockSpec((1, rows, rows), lambda h: (h, 0, 0))
    time_weights = call(
        time_weights_kernel,
        [head_block(3), mask_spec, mask_spec, shared((1, rows))],
        weights_spec,
        jax.ShapeDtypeStruct((head_count, rows, rows), F32),
        flops=2 * product,
        traffic=8 * size,
    )(moved, time_q_mask, time_k_mask, live_row)
    results = call(
        time_rest_kernel,
        [head_block(3), pl.BlockSpec((rows, HD), lambda h: (0, 2 * h)), weights_spec],
        head_block(3),
        jax.ShapeDtypeStruct((rows, 3 * channels), BF16),
        flops=4 * product,
        traffic=12 * size,
    )(moved, pair_moved, time_weights)
    back = exchange(results)

    grad_value_back = pair_moved.reshape(rows, head_count, 2, HD)[:, :, 1].reshape(rows, channels)
    grad_in = jnp.where(live_space[:, None], cotangent[0], jnp.zeros_like(cotangent[0]))
    grad_norm = grad_in.astype(F32) + grad_value_back.astype(F32)
    inner_norm = lax.psum(jnp.sum(grad_norm * normed_full, axis=-1), "head")
    grad_space_out = (
        inverse_rms[:, None] * (grad_norm - normed_full * (inner_norm / full_channels)[:, None])
    ).astype(BF16)
    grad_query_space, grad_key_space, grad_value_space = call(
        space_backward_kernel,
        [head_block()] * 4 + [mask_spec, mask_spec],
        [head_block()] * 3,
        [whole] * 3,
        flops=6 * product,
        traffic=7 * size,
    )(q_space, k_space, v_space, grad_space_out, space_q_mask, space_k_mask)

    mixed, grad_query_time, grad_key_time = call(
        finish_kernel,
        [head_block(3), head_block()],
        [head_block()] * 3,
        [whole] * 3,
        traffic=7 * size,
    )(back, normed)
    return (
        mixed[None],
        grad_query_space[None],
        grad_key_space[None],
        grad_value_space[None],
        grad_query_time[None],
        grad_key_time[None],
    )


def solution(mesh):
    sharded = P("frame", None, "head")
    return jax.shard_map(
        per_device,
        mesh=mesh,
        in_specs=(sharded,) * 6 + (P(), P()),
        out_specs=(sharded,) * 6,
        check_vma=False,
    )
```

time: 232 us -> 134 us (0.58)
  blocking collectives: 51.9 us -> 21.3 us
  matrix products: 29.6 us -> 0 us
  waiting for transfers between devices: 61.8 us -> 40.5 us
  Pallas kernels: 0 us -> 19.8 us
  starting transfers between devices: 45.6 us -> 29 us
  other arithmetic: 17.3 us -> 5.91 us
  local copies, waits for them, and re-layouts: 22 us -> 16.1 us
    all_to_all x1 -> x0, blocking collectives: 29 us -> none  [per_device(): lax.all_to_all(normed, 'frame', split_axis=1, concat_axis=0, tiled=True)]
    dot_general x11 -> x0, matrix products: 26.7 us -> none  [the longest x2 7.95 us: attend_backward(): jnp.einsum('bhqk,' + key_label + '->' + query_label, grad_scores, key_row...]
    all_to_all x7 -> x3, waiting for transfers between devices: 61.8 us -> 40.5 us  [exchange(): lax.all_to_all(blocks, 'frame', split_axis=0, concat_axis=0, tiled=True)]
    pallas_call x0 -> x7, Pallas kernels: none -> 19.8 us  [the longest x1 4.9 us: per_device(): call(space_backward_kernel, [head_block()] * 4 + [mask_spec, mask_spec],...]
    all_to_all x7 -> x3, starting transfers between devices: 45.6 us -> 29 us  [exchange(): lax.all_to_all(blocks, 'frame', split_axis=0, concat_axis=0, tiled=True)]
    unnamed x4 -> x0, other arithmetic: 12.3 us -> none
    unnamed x65 -> x36, local copies, waits for them, and re-layouts: 14.4 us -> 8.46 us
    sub x1 -> x0, matrix products: 2.96 us -> none  [attend_forward(): expanded = jnp.exp(scores - highest)]
  transfers between devices with their start and end apart: 7 -> 3, of which waited for: 5 -> 3; matrix products, arithmetic and copies ran while one was open for 19% -> 10% of each run, Pallas kernels for 0% -> 8%
where the time goes in v1:
time: 134 us
  waiting for transfers between devices  40.5 us (30%)
  starting transfers between devices  29 us (22%)
  blocking collectives  21.3 us (16%)
  Pallas kernels  19.8 us (15%)
  local copies, waits for them, and re-layouts  16.1 us (12%)
  other arithmetic  5.91 us (4%)
    all_to_all x3, waiting for transfers between devices, exchange(): lax.all_to_all(blocks, 'frame', split_axis=0, concat_axis=0, tiled=True)  40.5 us
    all_to_all x3, starting transfers between devices, exchange(): lax.all_to_all(blocks, 'frame', split_axis=0, concat_axis=0, tiled=True)  29 us
    psum x1, blocking collectives, per_device(): square_sum = lax.psum(jnp.sum(space_out * space_out, axis=-1), 'head')  10.7 us
    psum x1, blocking collectives, per_device(): inner_norm = lax.psum(jnp.sum(grad_norm * normed_full, axis=-1), 'head')  10.6 us
    unnamed x36, local copies, waits for them, and re-layouts  8.46 us
    pallas_call x1, Pallas kernels, per_device(): call(space_backward_kernel, [head_block()] * 4 + [mask_spec, mask_spec],...  4.9 us
    convert_element_type x2, local copies, waits for them, and re-layouts, per_device(): grad_norm = grad_in.astype(F32) + grad_value_back.astype(F32)  3.51 us
    pallas_call x1, Pallas kernels, per_device(): call(space_forward_kernel, [head_block()] * 3 + [mask_spec, mask_spec, sh...  3.19 us
  transfers between devices with their start and end apart: 3, of which 3 were waited for; matrix products, arithmetic and copies ran while one was open for 10% of the time, Pallas kernels for 8%

profile of v1, /device:TPU:6, one launch (start us, length us, event | category | flops | bytes accessed | tf_op | source)
XLA Modules:
  0.0 133.5 jit_solution(8904708094881885540)
XLA Ops:
  0.6 0.0 copy-start.3
  0.6 1.0 copy-done.3
  1.6 0.0 copy-start.8
  1.6 1.0 copy-done.8
  2.6 1.0 copy-done.9
  3.6 1.9 %shard_map.127 = bf16[512,1152]{1,0:T(8,128)(2,1)} custom-call(bf16[512,384]{1,0:T(8,128)(2,1)S(1)} %bitcast.30, bf16[512,384]{1,0:T(8,128)(2,1)S(1)} %bitcast.31, bf16[512,384]{1,0:T(8,128)(2,1)S(1)} %bitcast.28), custom_call_target="tpu_custom_call" | custom-call | bytes 2359296 | tf_op jit(solution)/shard_map/pallas_call | solution.py:148
  5.5 0.0 copy-start.14
  5.5 16.7 %all-to-all-start = ((bf16[64,8,1152]{2,1,0:T(8,128)(2,1)}), bf16[64,8,1152]{2,1,0:T(8,128)(2,1)S(1)}, u32[]{:S(2)}, u32[]{:S(2)}) async-start(bf16[64,8,1152]{2,1,0:T(8,128)(2,1)} %bitcast.3), calls=%async_computation | async-start | bytes 2359296 | tf_op jit(solution)/shard_map/all_to_all | solution.py:139
  22.3 0.0 copy-done.17
  22.3 0.1 iota_add_fusion
  22.4 0.1 add.53
  22.5 0.0 copy-done.16
  22.5 0.1 select_reduce_fusion
  22.6 0.6 dynamic_slice.3
  23.2 0.1 fusion.3
  23.2 0.1 lt.68
  23.3 0.1 reshape.132.live_ref
  23.4 0.7 select_convert_fusion.1
  24.1 0.7 fusion.2.live_ref
  24.8 0.1 broadcast_in_dim.87.k_mask_ref
  25.0 0.0 copy-done.10
  25.0 0.0 copy-done.12
  25.0 0.0 copy-done.14
  25.0 0.0 copy-start.6
  25.0 3.2 %shard_map.128 = f32[512,384]{1,0:T(8,128)S(1)} custom-call(bf16[512,384]{1,0:T(8,128)(2,1)S(1)} %bitcast.32, bf16[512,384]{1,0:T(8,128)(2,1)S(1)} %bitcast.34, bf16[512,384]{1,0:T(8,128)(2,1)S(1)} %bitcast.36, bf16[512,128]{1,0:T(8,128)(2,1)S(1)} %broadcast_in_dim.82.q_mask_ref, bf16[512,128]{1,0:T(8,128)(2,1)S(1)} %broadcast_in_dim.87.k_mask_ref, ...), custom_call_target="tpu_custom_call" | custom-call | flops 603979776 | bytes 1966080 | tf_op jit(solution)/shard_map/pallas_call | solution.py:175
  28.2 0.0 copy-done.6
  28.2 0.1 multiply_reduce_fusion.1
  28.4 10.7 %psum.14 = f32[512]{0:T(512)S(1)} all-reduce(f32[512]{0:T(512)S(1)} %multiply_reduce_fusion.1), channel_id=1, replica_groups=mesh['frame'=64,'head'=8] {'head'}, use_global_device_ids=true, to_apply=%region_2.3 | all-reduce | flops 512 | bytes 4096 | tf_op jit(solution)/shard_map/psum | solution.py:183
  39.1 0.1 fusion.1.q_mask_ref
  39.2 0.2 select_convert_fusion.k_mask_ref
  39.4 0.1 multiply_convert_fusion.1.normed_ref
  39.6 15.3 %all-to-all-done = bf16[64,8,1152]{2,1,0:T(8,128)(2,1)S(1)} async-done(((bf16[64,8,1152]{2,1,0:T(8,128)(2,1)}), bf16[64,8,1152]{2,1,0:T(8,128)(2,1)S(1)}, u32[]{:S(2)}, u32[]{:S(2)}) %all-to-all-start) | async-done | bytes 1179680 | tf_op jit(solution)/shard_map/all_to_all | solution.py:139
  54.9 2.8 %shard_map.129 = bf16[512,768]{1,0:T(8,128)(2,1)S(1)} custom-call(bf16[512,1152]{1,0:T(8,128)(2,1)S(1)} %bitcast.22, bf16[512,384]{1,0:T(8,128)(2,1)S(1)} %multiply_convert_fusion.1.normed_ref, bf16[512,128]{1,0:T(8,128)(2,1)S(1)} %fusion.1.q_mask_ref, bf16[512,128]{1,0:T(8,128)(2,1)S(1)} %select_convert_fusion.k_mask_ref, f32[1,512]{1,0:T(1,128)S(1)} %reshape.132.live_ref), custom_call_target="tpu_custom_call" | custom-call | flops 603979776 | bytes 2359296 | tf_op jit(solution)/shard_map/pallas_call | solution.py:188
  57.7 0.0 copy-start.5
  57.7 0.9 copy-done.5
  58.6 6.4 %all-to-all-start.1 = ((bf16[64,8,768]{2,1,0:T(8,128)(2,1)}), bf16[64,8,768]{2,1,0:T(8,128)(2,1)S(1)}, u32[]{:S(2)}, u32[]{:S(2)}) async-start(bf16[64,8,768]{2,1,0:T(8,128)(2,1)} %bitcast.29), calls=%async_computation.1 | async-start | bytes 1572864 | tf_op jit(solution)/shard_map/all_to_all | solution.py:139
  65.0 2.2 %shard_map.130.weights_ref = f32[3,512,512]{2,1,0:T(8,128)S(1)} custom-call(bf16[512,1152]{1,0:T(8,128)(2,1)S(1)} %bitcast.23, bf16[512,128]{1,0:T(8,128)(2,1)S(1)} %fusion.1.q_mask_ref, bf16[512,128]{1,0:T(8,128)(2,1)S(1)} %select_convert_fusion.k_mask_ref, f32[1,512]{1,0:T(1,128)S(1)} %reshape.132.live_ref), custom_call_target="tpu_custom_call" | custom-call | flops 402653184 | bytes 3145728 | tf_op jit(solution)/shard_map/pallas_call | solution.py:198
  67.2 0.0 copy-start
  67.2 1.6 %copy-done = f32[3,512,512]{2,1,0:T(8,128)} copy-done((f32[3,512,512]{2,1,0:T(8,128)}, f32[3,512,512]{2,1,0:T(8,128)S(1)}, u32[]{:S(2)}) %copy-start) | copy-done | bytes 3145752
  68.8 19.9 %all-to-all-done.1 = bf16[64,8,768]{2,1,0:T(8,128)(2,1)S(1)} async-done(((bf16[64,8,768]{2,1,0:T(8,128)(2,1)}), bf16[64,8,768]{2,1,0:T(8,128)(2,1)S(1)}, u32[]{:S(2)}, u32[]{:S(2)}) %all-to-all-start.1) | async-done | bytes 786464 | tf_op jit(solution)/shard_map/all_to_all | solution.py:139
  88.8 1.9 %copy-done.1 = f32[3,512,512]{2,1,0:T(8,128)S(1)} copy-done((f32[3,512,512]{2,1,0:T(8,128)S(1)}, f32[3,512,512]{2,1,0:T(8,128)}, u32[]{:S(2)}) %copy-start.1) | copy-done | bytes 3145752
  90.6 3.0 %shard_map.131 = bf16[512,1152]{1,0:T(8,128)(2,1)S(1)} custom-call(bf16[512,1152]{1,0:T(8,128)(2,1)S(1)} %bitcast.24, bf16[512,768]{1,0:T(8,128)(2,1)S(1)} %bitcast.25, f32[3,512,512]{2,1,0:T(8,128)S(1)} %copy-done.1), custom_call_target="tpu_custom_call" | custom-call | flops 805306368 | bytes 4718592 | tf_op jit(solution)/shard_map/pallas_call | solution.py:206
  93.7 0.0 copy-start.2
  93.7 1.0 copy-done.2
  94.7 5.9 %all-to-all-start.2 = ((bf16[64,8,1152]{2,1,0:T(8,128)(2,1)}), bf16[64,8,1152]{2,1,0:T(8,128)(2,1)S(1)}, u32[]{:S(2)}, u32[]{:S(2)}) async-start(bf16[64,8,1152]{2,1,0:T(8,128)(2,1)} %bitcast.27), calls=%async_computation.2 | async-start | bytes 2359296 | tf_op jit(solution)/shard_map/all_to_all | solution.py:139
  100.6 0.7 iota_compare_fusion.3
  101.3 1.1 reshape_reshape.3
  102.4 2.0 %slice.4 = bf16[512,3,1,128]{3,2,1,0:T(2,128)(2,1)S(1)} slice(bf16[512,3,2,128]{3,2,1,0:T(2,128)(2,1)} %reshape_reshape.3), slice={[0:512], [0:3], [1:2], [0:128]} | slice | bytes 786432 | tf_op jit(solution)/shard_map/slice | solution.py:216
  104.4 0.1 copy_convert_fusion
  104.4 1.2 copy.19
  105.6 2.3 %copy.20 = f32[512,384]{1,0:T(8,128)} copy(f32[512,384]{0,1:T(8,128)} %bitcast.38) | data formatting | bytes 1572864 | tf_op jit(solution)/shard_map/convert_element_type | solution.py:218
  107.9 0.0 copy-done.4
  107.9 1.5 %multiply_reduce_fusion = f32[512]{0:T(512)S(1)} fusion(f32[512,384]{1,0:T(8,128)S(1)} %shard_map.128, f32[512,384]{1,0:T(8,128)} %copy.20, f32[512]{0:T(512)S(1)} %add_rsqrt_fusion, pred[512]{0:T(512)(128)(4,1)S(1)} %iota_compare_fusion.3, bf16[1,512,384]{2,1,0:T(8,128)(2,1)S(1)} %copy-done.4), kind=kLoop, calls=%fused_computation.1 | loop fusion | flops 1179136 | bytes 1970688 | tf_op jit(solution)/shard_map/reduce_sum | solution.py:219
  109.4 10.6 %psum.15 = f32[512]{0:T(512)S(1)} all-reduce(f32[512]{0:T(512)S(1)} %multiply_reduce_fusion), channel_id=1, replica_groups=mesh['frame'=64,'head'=8] {'head'}, use_global_device_ids=true, to_apply=%region_4.5 | all-reduce | flops 512 | bytes 4096 | tf_op jit(solution)/shard_map/psum | solution.py:219
  120.0 0.0 copy-start.13
  120.1 0.0 copy-start.15
  120.1 1.5 %multiply_convert_fusion.g_ref = bf16[512,384]{1,0:T(8,128)(2,1)S(1)} fusion(f32[512,384]{1,0:T(8,128)S(1)} %shard_map.128, f32[512,384]{1,0:T(8,128)} %copy.20, f32[512]{0:T(512)S(1)} %broadcast_multiply_fusion, f32[512]{0:T(512)S(1)} %add_rsqrt_fusion, pred[512]{0:T(512)(128)(4,1)S(1)} %iota_compare_fusion.3, bf16[1,512,384]{2,1,0:T(8,128)(2,1)S(1)} %copy-done.4), kind=kLoop, calls=%fused_computation | loop fusion | flops 1572864 | bytes 2363904 | tf_op jit(solution)/shard_map/convert_element_type | solution.py:222
  121.6 0.0 copy-done.7
  121.6 0.0 copy-done.11
  121.6 0.0 copy-done.13
  121.6 0.0 copy-done.15
  121.6 4.9 %shard_map.133 = (bf16[512,384]{1,0:T(8,128)(2,1)}, bf16[512,384]{1,0:T(8,128)(2,1)}, bf16[512,384]{1,0:T(8,128)(2,1)}) custom-call(bf16[512,384]{1,0:T(8,128)(2,1)S(1)} %bitcast.33, bf16[512,384]{1,0:T(8,128)(2,1)S(1)} %bitcast.35, bf16[512,384]{1,0:T(8,128)(2,1)S(1)} %bitcast.37, bf16[512,384]{1,0:T(8,128)(2,1)S(1)} %multiply_convert_fusion.g_ref, ...), custom_call_target="tpu_custom_call" | custom-call | flops 1207959552 | bytes 2752512 | tf_op jit(solution)/shard_map/pallas_call | solution.py:223
  126.5 5.2 %all-to-all-done.2 = bf16[64,8,1152]{2,1,0:T(8,128)(2,1)S(1)} async-done(((bf16[64,8,1152]{2,1,0:T(8,128)(2,1)}), bf16[64,8,1152]{2,1,0:T(8,128)(2,1)S(1)}, u32[]{:S(2)}, u32[]{:S(2)}) %all-to-all-start.2) | async-done | bytes 1179680 | tf_op jit(solution)/shard_map/all_to_all | solution.py:139
  131.8 1.8 %shard_map.132 = (bf16[512,384]{1,0:T(8,128)(2,1)}, bf16[512,384]{1,0:T(8,128)(2,1)}, bf16[512,384]{1,0:T(8,128)(2,1)}) custom-call(bf16[512,1152]{1,0:T(8,128)(2,1)S(1)} %bitcast.26, bf16[512,384]{1,0:T(8,128)(2,1)S(1)} %multiply_convert_fusion.1.normed_ref), custom_call_target="tpu_custom_call" | custom-call | bytes 2752512 | tf_op jit(solution)/shard_map/pallas_call | solution.py:232
  (15 shorter events, 0.1 us)
Async XLA Ops:
  0.6 1.0 copy-start.3
  1.6 1.0 copy-start.8
  2.6 1.0 copy-start.9
  5.5 16.8 %copy-start.17 = (s32[64]{0:T(128)S(1)}, s32[64]{0:T(128)}, u32[]{:S(2)}) copy-start(s32[64]{0:T(128)} %param.14) | copy-start | bytes 772
  5.5 17.0 %copy-start.16 = (s32[6]{0:T(128)S(1)}, s32[6]{0:T(128)}, u32[]{:S(2)}) copy-start(s32[6]{0:T(128)} %param.15) | copy-start | bytes 76
  5.5 19.4 %copy-start.10 = (bf16[1,512,384]{2,1,0:T(8,128)(2,1)S(1)}, bf16[1,512,384]{2,1,0:T(8,128)(2,1)}, u32[]{:S(2)}) copy-start(bf16[1,512,384]{2,1,0:T(8,128)(2,1)} %param.8) | copy-start | bytes 1179652
  5.5 19.4 %copy-start.12 = (bf16[1,512,384]{2,1,0:T(8,128)(2,1)S(1)}, bf16[1,512,384]{2,1,0:T(8,128)(2,1)}, u32[]{:S(2)}) copy-start(bf16[1,512,384]{2,1,0:T(8,128)(2,1)} %param.9) | copy-start | bytes 1179652
  5.5 19.4 %copy-start.14 = (bf16[1,512,384]{2,1,0:T(8,128)(2,1)S(1)}, bf16[1,512,384]{2,1,0:T(8,128)(2,1)}, u32[]{:S(2)}) copy-start(bf16[1,512,384]{2,1,0:T(8,128)(2,1)} %param.10) | copy-start | bytes 1179652
  5.5 49.4 %all-to-all-start = ((bf16[64,8,1152]{2,1,0:T(8,128)(2,1)}), bf16[64,8,1152]{2,1,0:T(8,128)(2,1)S(1)}, u32[]{:S(2)}, u32[]{:S(2)}) async-start(bf16[64,8,1152]{2,1,0:T(8,128)(2,1)} %bitcast.3), calls=%async_computation | async-start | bytes 2359296 | tf_op jit(solution)/shard_map/all_to_all | solution.py:139
  25.0 3.2 %copy-start.6 = (bf16[512,128]{1,0:T(8,128)(2,1)}, bf16[512,128]{1,0:T(8,128)(2,1)S(1)}, u32[]{:S(2)}) copy-start(bf16[512,128]{1,0:T(8,128)(2,1)S(1)} %broadcast_in_dim.87.k_mask_ref) | copy-start | bytes 393220
  57.7 0.9 copy-start.5
  58.6 30.1 %all-to-all-start.1 = ((bf16[64,8,768]{2,1,0:T(8,128)(2,1)}), bf16[64,8,768]{2,1,0:T(8,128)(2,1)S(1)}, u32[]{:S(2)}, u32[]{:S(2)}) async-start(bf16[64,8,768]{2,1,0:T(8,128)(2,1)} %bitcast.29), calls=%async_computation.1 | async-start | bytes 1572864 | tf_op jit(solution)/shard_map/all_to_all | solution.py:139
  67.2 1.6 %copy-start = (f32[3,512,512]{2,1,0:T(8,128)}, f32[3,512,512]{2,1,0:T(8,128)S(1)}, u32[]{:S(2)}) copy-start(f32[3,512,512]{2,1,0:T(8,128)S(1)} %shard_map.130.weights_ref) | copy-start | bytes 9437188
  88.8 1.9 %copy-start.1 = (f32[3,512,512]{2,1,0:T(8,128)S(1)}, f32[3,512,512]{2,1,0:T(8,128)}, u32[]{:S(2)}) copy-start(f32[3,512,512]{2,1,0:T(8,128)} %copy-done) | copy-start | bytes 9437188
  93.7 1.0 copy-start.2
  94.7 37.1 %all-to-all-start.2 = ((bf16[64,8,1152]{2,1,0:T(8,128)(2,1)}), bf16[64,8,1152]{2,1,0:T(8,128)(2,1)S(1)}, u32[]{:S(2)}, u32[]{:S(2)}) async-start(bf16[64,8,1152]{2,1,0:T(8,128)(2,1)} %bitcast.27), calls=%async_computation.2 | async-start | bytes 2359296 | tf_op jit(solution)/shard_map/all_to_all | solution.py:139
  105.6 2.4 %copy-start.4 = (bf16[1,512,384]{2,1,0:T(8,128)(2,1)S(1)}, bf16[1,512,384]{2,1,0:T(8,128)(2,1)}, u32[]{:S(2)}) copy-start(bf16[1,512,384]{2,1,0:T(8,128)(2,1)} %param.13) | copy-start | bytes 1179652
  120.0 1.6 %copy-start.7 = (bf16[512,128]{1,0:T(8,128)(2,1)S(1)}, bf16[512,128]{1,0:T(8,128)(2,1)}, u32[]{:S(2)}) copy-start(bf16[512,128]{1,0:T(8,128)(2,1)} %copy-done.6) | copy-start | bytes 393220
  120.0 1.6 %copy-start.11 = (bf16[1,512,384]{2,1,0:T(8,128)(2,1)S(1)}, bf16[1,512,384]{2,1,0:T(8,128)(2,1)}, u32[]{:S(2)}) copy-start(bf16[1,512,384]{2,1,0:T(8,128)(2,1)} %param.8) | copy-start | bytes 1179652
  120.0 1.6 %copy-start.13 = (bf16[1,512,384]{2,1,0:T(8,128)(2,1)S(1)}, bf16[1,512,384]{2,1,0:T(8,128)(2,1)}, u32[]{:S(2)}) copy-start(bf16[1,512,384]{2,1,0:T(8,128)(2,1)} %param.9) | copy-start | bytes 1179652
  120.1 1.6 %copy-start.15 = (bf16[1,512,384]{2,1,0:T(8,128)(2,1)S(1)}, bf16[1,512,384]{2,1,0:T(8,128)(2,1)}, u32[]{:S(2)}) copy-start(bf16[1,512,384]{2,1,0:T(8,128)(2,1)} %param.10) | copy-start | bytes 1179652

commit v2 on v1

--- a/solution.py
+++ b/solution.py
@@ -11,7 +11,8 @@
 LOG2E = 1.4426950408889634
 F32 = jnp.float32
 BF16 = jnp.bfloat16
-VMEM_BYTES = 32 * 1024 * 1024
+VMEM_BYTES = 24 * 1024 * 1024
+LOWEST = -3e38
 
 
 def dot(a, b, ca, cb):
@@ -38,10 +39,23 @@
     return expanded, 1.0 / jnp.sum(expanded, axis=1, keepdims=True)
 
 
-def pack_kernel(a_ref, b_ref, c_ref, out_ref):
-    out_ref[:, :HD] = a_ref[...]
-    out_ref[:, HD : 2 * HD] = b_ref[...]
-    out_ref[:, 2 * HD :] = c_ref[...]
+def pack_kernel(a_ref, b_ref, c_ref, out_ref, held, in_sem, out_sem):
+    width = a_ref.shape[1]
+    loads, stores = [], []
+    for i, ref in enumerate((a_ref, b_ref, c_ref)):
+        loads.append(pltpu.make_async_copy(ref, held.at[i], in_sem.at[i]))
+        stores.append(
+            pltpu.make_async_copy(
+                held.at[i], out_ref.at[:, pl.ds(i * width, width)], out_sem.at[i]
+            )
+        )
+    for load in loads:
+        load.start()
+    for load, store in zip(loads, stores):
+        load.wait()
+        store.start()
+    for store in stores:
+        store.wait()
 
 
 def space_forward_kernel(q_ref, k_ref, v_ref, q_mask_ref, k_mask_ref, live_ref, out_ref):
@@ -67,39 +81,88 @@
     gq_ref[...] = dot(grad_scores, k, 0, 0).astype(BF16)
 
 
-def time_value_kernel(moved_ref, normed_ref, q_mask_ref, k_mask_ref, live_ref, out_ref):
-    q, k, g = moved_ref[:, :HD], moved_ref[:, HD : 2 * HD], moved_ref[:, 2 * HD :]
-    expanded, inverse = softmax_keys_first(q, k, q_mask_ref[...], k_mask_ref[...])
-    weights = (expanded * (inverse * live_ref[...])).astype(BF16)
-    out_ref[:, :HD] = normed_ref[...]
-    out_ref[:, HD:] = dot(weights, g, 1, 0).astype(BF16)
-
-
-def time_weights_kernel(moved_ref, q_mask_ref, k_mask_ref, live_ref, weights_ref):
-    q, k = moved_ref[:, :HD], moved_ref[:, HD : 2 * HD]
-    expanded, inverse = softmax_keys_first(q, k, q_mask_ref[...], k_mask_ref[...])
-    weights_ref[0] = expanded * (inverse * live_ref[...])
-
-
-def time_rest_kernel(moved_ref, normed_ref, weights_ref, out_ref):
+def time_value_kernel(
+    moved_ref, normed_ref, q_mask_ref, k_mask_ref, live_ref, out_ref, shift_ref, held, sem
+):
+    scale = HD ** (-0.5) * LOG2E
+    width = normed_ref.shape[1]
+    heads = width // HD
+    copies = [pltpu.make_async_copy(normed_ref, out_ref.at[:, pl.ds(0, width)], sem.at[heads])]
+    copies[0].start()
+    q_mask, k_mask, live = q_mask_ref[...], k_mask_ref[...], live_ref[...]
+    for h in range(heads):
+        q, k, g = (
+            moved_ref[:, j * width + h * HD : j * width + (h + 1) * HD] for j in range(3)
+        )
+        scores = dot(
+            jnp.concatenate([k, k_mask], axis=1), jnp.concatenate([q, q_mask], axis=1), 1, 1
+        )
+        highest = jnp.max(scores, axis=0, keepdims=True)
+        expanded = jnp.exp2((scores - highest) * scale)
+        inverse = 1.0 / jnp.sum(expanded, axis=0, keepdims=True)
+        weights = (expanded * (inverse * live)).astype(BF16)
+        shift_ref[h : h + 1, :] = jnp.where(
+            live > 0, jnp.log2(inverse) - highest * scale, LOWEST
+        )
+        held[h] = dot(weights, g, 1, 0).astype(BF16)
+        copies.append(
+            pltpu.make_async_copy(
+                held.at[h], out_ref.at[:, pl.ds(width + h * HD, HD)], sem.at[h]
+            )
+        )
+        copies[-1].start()
+    for copy in copies:
+        copy.wait()
+
+
+def time_rest_kernel(
+    moved_ref, pair_ref, q_mask_ref, k_mask_ref, shift_ref, out_ref, held, sem
+):
     scale = HD ** (-0.5)
-    q, k, g = moved_ref[:, :HD], moved_ref[:, HD : 2 * HD], moved_ref[:, 2 * HD :]
-    v = normed_ref[...]
-    weights = weights_ref[0]
-    out_ref[:, :HD] = dot(weights.astype(BF16), v, 0, 0).astype(BF16)
-    grad_weights = dot(v, g, 1, 1)
-    inner = jnp.sum(weights * grad_weights, axis=0, keepdims=True)
-    grad_scores = (weights * (grad_weights - inner) * scale).astype(BF16)
-    out_ref[:, HD : 2 * HD] = dot(grad_scores, k, 0, 0).astype(BF16)
-    out_ref[:, 2 * HD :] = dot(grad_scores, q, 1, 0).astype(BF16)
-
-
-def finish_kernel(back_ref, normed_ref, mixed_ref, gq_ref, gk_ref):
-    mixed_ref[...] = (
-        normed_ref[...].astype(F32) + back_ref[:, :HD].astype(F32)
-    ).astype(BF16)
-    gq_ref[...] = back_ref[:, HD : 2 * HD]
-    gk_ref[...] = back_ref[:, 2 * HD :]
+    width = pair_ref.shape[1] // 2
+    heads = width // HD
+    copies = []
+    q_mask, k_mask = q_mask_ref[...], k_mask_ref[...]
+    for h in range(heads):
+        q, k, g = (
+            moved_ref[:, j * width + h * HD : j * width + (h + 1) * HD] for j in range(3)
+        )
+        v = pair_ref[:, h * HD : (h + 1) * HD]
+        scores = dot(
+            jnp.concatenate([k, k_mask], axis=1), jnp.concatenate([q, q_mask], axis=1), 1, 1
+        )
+        weights = jnp.exp2(scores * (scale * LOG2E) + shift_ref[h : h + 1, :])
+        time_out = dot(weights.astype(BF16), v, 0, 0)
+        grad_weights = dot(v, g, 1, 1)
+        inner = jnp.sum(weights * grad_weights, axis=0, keepdims=True)
+        grad_scores = (weights * (grad_weights - inner)).astype(BF16)
+        grad_query = dot(grad_scores, k, 0, 0) * scale
+        grad_key = dot(grad_scores, q, 1, 0) * scale
+        for j, result in enumerate((time_out, grad_query, grad_key)):
+            held[j, h] = result.astype(BF16)
+            copies.append(
+                pltpu.make_async_copy(
+                    held.at[j, h], out_ref.at[:, pl.ds(j * width + h * HD, HD)], sem.at[j, h]
+                )
+            )
+            copies[-1].start()
+    for copy in copies:
+        copy.wait()
+
+
+def finish_kernel(back_ref, normed_ref, mixed_ref, gq_ref, gk_ref, held, sem):
+    width = normed_ref.shape[1]
+    copies = [
+        pltpu.make_async_copy(back_ref.at[:, pl.ds(width, width)], gq_ref, sem.at[0]),
+        pltpu.make_async_copy(back_ref.at[:, pl.ds(2 * width, width)], gk_ref, sem.at[1]),
+        pltpu.make_async_copy(held, mixed_ref, sem.at[2]),
+    ]
+    copies[0].start()
+    copies[1].start()
+    held[...] = (normed_ref[...].astype(F32) + back_ref[:, :width].astype(F32)).astype(BF16)
+    copies[2].start()
+    for copy in copies:
+        copy.wait()
 
 
 def per_device(
@@ -111,6 +174,7 @@
     full_channels = channels * lax.axis_size("head")
     positions_here = rows // lax.axis_size("frame")
     here = lax.axis_index("frame")
+    side = 8
 
     def head_block(width=1):
         return pl.BlockSpec((rows, width * HD), lambda h: (0, h))
@@ -133,10 +197,31 @@
             ),
         )
 
+    def local(kernel, in_specs, out_specs, out_shape, scratch, flops=0, traffic=0):
+        return pl.pallas_call(
+            kernel,
+            in_specs=in_specs,
+            out_specs=out_specs,
+            out_shape=out_shape,
+            scratch_shapes=scratch,
+            compiler_params=pltpu.CompilerParams(vmem_limit_bytes=VMEM_BYTES),
+            cost_estimate=pl.CostEstimate(
+                flops=flops, bytes_accessed=traffic, transcendentals=0
+            ),
+        )
+
+    order = [z * side + y for y in range(side) for z in range(side)]
+    block_here = lax.rem(here, side) * side + lax.div(here, side)
+
+    def ordered(per_frame):
+        return per_frame.reshape(side, side).T.reshape(frames)
+
     def exchange(array):
         width = array.shape[-1]
         blocks = array.reshape(frames, positions_here, width)
-        moved = lax.all_to_all(blocks, "frame", split_axis=0, concat_axis=0, tiled=True)
+        moved = lax.all_to_all(
+            blocks, "frame", split_axis=0, concat_axis=0, tiled=True, axis_index_groups=[order]
+        )
         return moved.reshape(rows, width)
 
     whole = jax.ShapeDtypeStruct((rows, channels), BF16)
@@ -145,11 +230,14 @@
 
     q_space, k_space, v_space = query_space[0], key_space[0], value_space[0]
 
-    packed = call(
+    hbm, vmem = pl.BlockSpec(memory_space=pltpu.HBM), pl.BlockSpec(memory_space=pltpu.VMEM)
+    dma = pltpu.SemaphoreType.DMA
+    packed = local(
         pack_kernel,
-        [head_block()] * 3,
-        head_block(3),
+        [hbm] * 3,
+        hbm,
         jax.ShapeDtypeStruct((rows, 3 * channels), BF16),
+        [pltpu.VMEM((3, rows, channels), BF16), dma((3,)), dma((3,))],
         traffic=6 * size,
     )(query_time[0], key_time[0], cotangent[0])
     moved = exchange(packed)
@@ -163,8 +251,8 @@
     space_k_mask = jnp.where(live_space[:, None], 0.0, NEGATIVE).astype(BF16)
     space_k_mask = jnp.broadcast_to(space_k_mask, (rows, HD))
     place = jnp.arange(positions_here, dtype=jnp.int32)[None, :]
-    live_time = (here * positions_here + place) < slot_res[:, None]
-    group = slot_clip[:, None] * positions_here + place
+    live_time = (block_here * positions_here + place) < ordered(slot_res)[:, None]
+    group = ordered(slot_clip)[:, None] * positions_here + place
     group = group.reshape(rows, 1)
     time_q_mask = (column == group).astype(BF16)
     time_k_mask = jnp.where((column == group) & live_time.reshape(rows, 1), 0.0, NEGATIVE)
@@ -185,35 +273,31 @@
     normed_full = space_out * inverse_rms[:, None]
     normed = normed_full.astype(BF16)
 
-    pair = call(
+    pair, shift = local(
         time_value_kernel,
-        [head_block(3), head_block(), mask_spec, mask_spec, shared((1, rows))],
-        head_block(2),
-        jax.ShapeDtypeStruct((rows, 2 * channels), BF16),
+        [vmem] * 5,
+        [hbm, vmem],
+        [
+            jax.ShapeDtypeStruct((rows, 2 * channels), BF16),
+            jax.ShapeDtypeStruct((8, rows), F32),
+        ],
+        [pltpu.VMEM((head_count, rows, HD), BF16), dma((head_count + 1,))],
         flops=3 * product,
         traffic=6 * size,
     )(moved, normed, time_q_mask, time_k_mask, live_row)
     pair_moved = exchange(pair)
-    weights_spec = pl.BlockSpec((1, rows, rows), lambda h: (h, 0, 0))
-    time_weights = call(
-        time_weights_kernel,
-        [head_block(3), mask_spec, mask_spec, shared((1, rows))],
-        weights_spec,
-        jax.ShapeDtypeStruct((head_count, rows, rows), F32),
-        flops=2 * product,
+    results = local(
+        time_rest_kernel,
+        [vmem] * 5,
+        hbm,
+        jax.ShapeDtypeStruct((rows, 3 * channels), BF16),
+        [pltpu.VMEM((3, head_count, rows, HD), BF16), dma((3, head_count))],
+        flops=6 * product,
         traffic=8 * size,
-    )(moved, time_q_mask, time_k_mask, live_row)
-    results = call(
-        time_rest_kernel,
-        [head_block(3), pl.BlockSpec((rows, HD), lambda h: (0, 2 * h)), weights_spec],
-        head_block(3),
-        jax.ShapeDtypeStruct((rows, 3 * channels), BF16),
-        flops=4 * product,
-        traffic=12 * size,
-    )(moved, pair_moved, time_weights)
+    )(moved, pair_moved, time_q_mask, time_k_mask, shift)
     back = exchange(results)
 
-    grad_value_back = pair_moved.reshape(rows, head_count, 2, HD)[:, :, 1].reshape(rows, channels)
+    grad_value_back = pair_moved[:, channels:]
     grad_in = jnp.where(live_space[:, None], cotangent[0], jnp.zeros_like(cotangent[0]))
     grad_norm = grad_in.astype(F32) + grad_value_back.astype(F32)
     inner_norm = lax.psum(jnp.sum(grad_norm * normed_full, axis=-1), "head")
@@ -229,11 +313,12 @@
         traffic=7 * size,
     )(q_space, k_space, v_space, grad_space_out, space_q_mask, space_k_mask)
 
-    mixed, grad_query_time, grad_key_time = call(
+    mixed, grad_query_time, grad_key_time = local(
         finish_kernel,
-        [head_block(3), head_block()],
-        [head_block()] * 3,
+        [vmem] * 2,
+        [hbm] * 3,
         [whole] * 3,
+        [pltpu.VMEM((rows, channels), BF16), dma((3,))],
         traffic=7 * size,
     )(back, normed)
     return (

time: 134 us -> 133 us (level)
  blocking collectives: 21.3 us -> 51.5 us
  waiting for transfers between devices: 40.5 us -> 28.6 us
  local copies, waits for them, and re-layouts: 16.1 us -> 6.54 us
  starting transfers between devices: 29 us -> 23.2 us
  Pallas kernels: 19.8 us -> 17.2 us
  other arithmetic: 5.91 us -> 3.59 us
    all_to_all x0 -> x1, blocking collectives: none -> 30.2 us  [exchange(): lax.all_to_all(blocks, 'frame', split_axis=0, concat_axis=0, tiled=True,...]
    all_to_all x3 -> x2, waiting for transfers between devices: 40.5 us -> 28.6 us  [exchange(): lax.all_to_all(blocks, 'frame', split_axis=0, concat_axis=0, tiled=True,...]
    all_to_all x3 -> x2, starting transfers between devices: 29 us -> 23.2 us  [exchange(): lax.all_to_all(blocks, 'frame', split_axis=0, concat_axis=0, tiled=True,...]
    convert_element_type x2 -> x0, local copies, waits for them, and re-layouts: 3.51 us -> none  [per_device(): grad_norm = grad_in.astype(F32) + grad_value_back.astype(F32)]
    unnamed x36 -> x34, local copies, waits for them, and re-layouts: 8.46 us -> 5.05 us
    pallas_call x5 -> x4, Pallas kernels: 11.7 us -> 9.17 us  [the longest x1 3.66 us: per_device(): local(time_rest_kernel, [vmem] * 5, hbm, jax.ShapeDtypeStruct((rows, 3 *...]
    slice x1 -> x0, local copies, waits for them, and re-layouts: 2.01 us -> none  [per_device(): pair_moved.reshape(rows, head_count, 2, HD)[:, :, 1].reshape(rows, channels)]
  transfers between devices with their start and end apart: 3 -> 2, of which waited for: 3 -> 2; matrix products, arithmetic and copies ran while one was open for 10% -> 4% of each run, Pallas kernels for 8% -> 6%
where the time goes in v2:
time: 133 us; the launch traced here: 132 us
  blocking collectives  51.5 us (39%)
  waiting for transfers between devices  28.6 us (22%)
  starting transfers between devices  23.2 us (17%)
  Pallas kernels  17.2 us (13%)
  local copies, waits for them, and re-layouts  6.54 us (5%)
  other arithmetic  3.59 us (3%)
    all_to_all x1, blocking collectives, exchange(): lax.all_to_all(blocks, 'frame', split_axis=0, concat_axis=0, tiled=True,...  30.2 us
    all_to_all x2, waiting for transfers between devices, exchange(): lax.all_to_all(blocks, 'frame', split_axis=0, concat_axis=0, tiled=True,...  28.6 us
    all_to_all x2, starting transfers between devices, exchange(): lax.all_to_all(blocks, 'frame', split_axis=0, concat_axis=0, tiled=True,...  23.2 us
    psum x1, blocking collectives, per_device(): square_sum = lax.psum(jnp.sum(space_out * space_out, axis=-1), 'head')  10.7 us
    psum x1, blocking collectives, per_device(): inner_norm = lax.psum(jnp.sum(grad_norm * normed_full, axis=-1), 'head')  10.6 us
    unnamed x34, local copies, waits for them, and re-layouts  5.05 us
    pallas_call x1, Pallas kernels, per_device(): call(space_backward_kernel, [head_block()] * 4 + [mask_spec, mask_spec],...  4.88 us
    pallas_call x1, Pallas kernels, per_device(): local(time_rest_kernel, [vmem] * 5, hbm, jax.ShapeDtypeStruct((rows, 3 *...  3.66 us
  transfers between devices with their start and end apart: 2, of which 2 were waited for; matrix products, arithmetic and copies ran while one was open for 4% of the time, Pallas kernels for 6%

profile of v2, /device:TPU:6, one launch (start us, length us, event | category | flops | bytes accessed | tf_op | source)
XLA Modules:
  0.0 131.7 jit_solution(18193393747657437494)
XLA Ops:
  0.6 0.0 copy-start
  0.6 1.0 copy-done
  1.6 1.0 copy-done.7
  2.6 1.0 copy-done.8
  3.6 1.7 %shard_map.127 = bf16[512,1152]{1,0:T(8,128)(2,1)} custom-call(bf16[512,384]{1,0:T(8,128)(2,1)S(1)} %bitcast.32, bf16[512,384]{1,0:T(8,128)(2,1)S(1)} %bitcast.33, bf16[512,384]{1,0:T(8,128)(2,1)S(1)} %bitcast.24), custom_call_target="tpu_custom_call" | custom-call | bytes 2359296 | tf_op jit(solution)/shard_map/pallas_call | solution.py:235
  5.3 0.0 copy-start.15
  5.3 0.0 copy-start.16
  5.3 0.0 copy-start.9
  5.4 0.0 copy-start.11
  5.4 0.0 copy-start.13
  5.4 16.7 %all-to-all-start = ((bf16[64,8,1152]{2,1,0:T(8,128)(2,1)}), bf16[64,8,1152]{2,1,0:T(8,128)(2,1)S(1)}, u32[]{:S(2)}, u32[]{:S(2)}) async-start(bf16[64,8,1152]{2,1,0:T(8,128)(2,1)} %bitcast.3), calls=%async_computation | async-start | bytes 2359296 | tf_op jit(solution)/shard_map/all_to_all | solution.py:222
  22.1 0.0 copy-done.15
  22.1 0.0 copy-done.16
  22.2 0.1 select_reduce_fusion
  22.2 0.1 reshape.139
  22.3 0.6 dynamic_slice.3
  22.9 0.1 mul.59
  23.0 0.1 copy.18
  23.1 0.1 mul.61
  23.1 0.1 copy.19
  23.2 0.1 lt.68
  23.3 0.1 iota_add_fusion
  23.4 0.1 add.56
  23.5 0.1 fusion.3
  23.6 0.1 reshape.144.live_ref
  23.7 0.1 lt.71
  23.8 0.7 select_convert_fusion.1
  24.4 0.7 fusion.2.live_ref
  25.1 0.1 broadcast_in_dim.85.k_mask_ref
  25.3 0.0 copy-start.3
  25.3 0.0 copy-done.9
  25.3 0.0 copy-done.11
  25.3 0.0 copy-done.13
  25.3 0.0 copy-start.5
  25.3 3.2 %shard_map.128 = f32[512,384]{1,0:T(8,128)S(1)} custom-call(bf16[512,384]{1,0:T(8,128)(2,1)S(1)} %bitcast.34, bf16[512,384]{1,0:T(8,128)(2,1)S(1)} %bitcast.36, bf16[512,384]{1,0:T(8,128)(2,1)S(1)} %bitcast.38, bf16[512,128]{1,0:T(8,128)(2,1)S(1)} %broadcast_in_dim.80.q_mask_ref, bf16[512,128]{1,0:T(8,128)(2,1)S(1)} %broadcast_in_dim.85.k_mask_ref, ...), custom_call_target="tpu_custom_call" | custom-call | flops 603979776 | bytes 1966080 | tf_op jit(solution)/shard_map/pallas_call | solution.py:263
  28.5 0.0 copy-done.3
  28.5 0.0 copy-done.5
  28.6 0.1 multiply_reduce_fusion.1
  28.7 10.7 %psum.14 = f32[512]{0:T(512)S(1)} all-reduce(f32[512]{0:T(512)S(1)} %multiply_reduce_fusion.1), channel_id=1, replica_groups=mesh['frame'=64,'head'=8] {'head'}, use_global_device_ids=true, to_apply=%region_2.3 | all-reduce | flops 512 | bytes 4096 | tf_op jit(solution)/shard_map/psum | solution.py:271
  39.4 0.1 fusion.1.q_mask_ref
  39.6 0.2 select_convert_fusion.k_mask_ref
  39.8 0.1 multiply_convert_fusion.1.normed_ref
  39.9 14.4 %all-to-all-done = bf16[64,8,1152]{2,1,0:T(8,128)(2,1)S(1)} async-done(((bf16[64,8,1152]{2,1,0:T(8,128)(2,1)}), bf16[64,8,1152]{2,1,0:T(8,128)(2,1)S(1)}, u32[]{:S(2)}, u32[]{:S(2)}) %all-to-all-start) | async-done | bytes 1179680 | tf_op jit(solution)/shard_map/all_to_all | solution.py:222
  54.4 2.8 %shard_map.129 = (bf16[512,768]{1,0:T(8,128)(2,1)S(1)}, f32[8,512]{1,0:T(8,128)S(1)}) custom-call(bf16[512,1152]{1,0:T(8,128)(2,1)S(1)} %bitcast.28, bf16[512,384]{1,0:T(8,128)(2,1)S(1)} %multiply_convert_fusion.1.normed_ref, bf16[512,128]{1,0:T(8,128)(2,1)S(1)} %fusion.1.q_mask_ref, bf16[512,128]{1,0:T(8,128)(2,1)S(1)} %select_convert_fusion.k_mask_ref, ...), custom_call_target="tpu_custom_call" | custom-call | flops 603979776 | bytes 2359296 | tf_op jit(solution)/shard_map/pallas_call | solution.py:276
  57.1 30.2 %all_to_all.15 = bf16[64,8,768]{2,1,0:T(8,128)(2,1)S(1)} all-to-all(bf16[64,8,768]{2,1,0:T(8,128)(2,1)S(1)} %bitcast.31), channel_id=1, replica_groups={{0,64,128,192,256,320,384,448,8,72,136,200,264,328,392,456,16,80,144,20..., dimensions={0} | all-to-all | bytes 1572864 | tf_op jit(solution)/shard_map/all_to_all | solution.py:222
  87.4 3.7 %shard_map.130 = bf16[512,1152]{1,0:T(8,128)(2,1)S(1)} custom-call(bf16[512,1152]{1,0:T(8,128)(2,1)S(1)} %bitcast.29, bf16[512,768]{1,0:T(8,128)(2,1)S(1)} %bitcast.25, bf16[512,128]{1,0:T(8,128)(2,1)S(1)} %fusion.1.q_mask_ref, bf16[512,128]{1,0:T(8,128)(2,1)S(1)} %select_convert_fusion.k_mask_ref, f32[8,512]{1,0:T(8,128)S(1)} %get-tuple-element.15.shift_ref), custom_call_target="tpu_custom_call" | custom-call | flops 1207959552 | bytes 3145728 | tf_op jit(solution)/shard_map/pallas_call | solution.py:289
  91.0 0.0 copy-start.2
  91.0 1.0 copy-done.2
  92.0 6.5 %all-to-all-start.2 = ((bf16[64,8,1152]{2,1,0:T(8,128)(2,1)}), bf16[64,8,1152]{2,1,0:T(8,128)(2,1)S(1)}, u32[]{:S(2)}, u32[]{:S(2)}) async-start(bf16[64,8,1152]{2,1,0:T(8,128)(2,1)} %bitcast.30), calls=%async_computation.2 | async-start | bytes 2359296 | tf_op jit(solution)/shard_map/all_to_all | solution.py:222
  98.5 0.7 iota_compare_fusion.3
  99.2 0.4 multiply_reduce_fusion
  99.6 10.6 %psum.15 = f32[512]{0:T(512)S(1)} all-reduce(f32[512]{0:T(512)S(1)} %multiply_reduce_fusion), channel_id=1, replica_groups=mesh['frame'=64,'head'=8] {'head'}, use_global_device_ids=true, to_apply=%region_4.5 | all-reduce | flops 512 | bytes 4096 | tf_op jit(solution)/shard_map/psum | solution.py:303
  110.2 0.0 copy-start.10
  110.2 0.0 copy-start.12
  110.2 0.0 copy-start.14
  110.2 0.3 multiply_convert_fusion.g_ref
  110.6 0.5 copy-done.4
  111.1 0.1 copy-done.6
  111.2 0.2 copy-done.10
  111.3 0.1 copy-done.12
  111.4 0.1 copy-done.14
  111.6 4.9 %shard_map.132 = (bf16[512,384]{1,0:T(8,128)(2,1)}, bf16[512,384]{1,0:T(8,128)(2,1)}, bf16[512,384]{1,0:T(8,128)(2,1)}) custom-call(bf16[512,384]{1,0:T(8,128)(2,1)S(1)} %bitcast.35, bf16[512,384]{1,0:T(8,128)(2,1)S(1)} %bitcast.37, bf16[512,384]{1,0:T(8,128)(2,1)S(1)} %bitcast.39, bf16[512,384]{1,0:T(8,128)(2,1)S(1)} %multiply_convert_fusion.g_ref, ...), custom_call_target="tpu_custom_call" | custom-call | flops 1207959552 | bytes 2752512 | tf_op jit(solution)/shard_map/pallas_call | solution.py:307
  116.4 14.2 %all-to-all-done.2 = bf16[64,8,1152]{2,1,0:T(8,128)(2,1)S(1)} async-done(((bf16[64,8,1152]{2,1,0:T(8,128)(2,1)}), bf16[64,8,1152]{2,1,0:T(8,128)(2,1)S(1)}, u32[]{:S(2)}, u32[]{:S(2)}) %all-to-all-start.2) | async-done | bytes 1179680 | tf_op jit(solution)/shard_map/all_to_all | solution.py:222
  130.6 1.0 shard_map.131
  (12 shorter events, 0.1 us)
Async XLA Ops:
  0.6 1.0 copy-start
  1.6 1.0 copy-start.7
  2.6 1.0 copy-start.8
  5.3 16.8 %copy-start.15 = (s32[6]{0:T(128)S(1)}, s32[6]{0:T(128)}, u32[]{:S(2)}) copy-start(s32[6]{0:T(128)} %param.15) | copy-start | bytes 76
  5.3 16.8 %copy-start.16 = (s32[64]{0:T(128)S(1)}, s32[64]{0:T(128)}, u32[]{:S(2)}) copy-start(s32[64]{0:T(128)} %param.14) | copy-start | bytes 772
  5.3 19.9 %copy-start.9 = (bf16[1,512,384]{2,1,0:T(8,128)(2,1)S(1)}, bf16[1,512,384]{2,1,0:T(8,128)(2,1)}, u32[]{:S(2)}) copy-start(bf16[1,512,384]{2,1,0:T(8,128)(2,1)} %param.8) | copy-start | bytes 1179652
  5.4 19.9 %copy-start.11 = (bf16[1,512,384]{2,1,0:T(8,128)(2,1)S(1)}, bf16[1,512,384]{2,1,0:T(8,128)(2,1)}, u32[]{:S(2)}) copy-start(bf16[1,512,384]{2,1,0:T(8,128)(2,1)} %param.9) | copy-start | bytes 1179652
  5.4 19.9 %copy-start.13 = (bf16[1,512,384]{2,1,0:T(8,128)(2,1)S(1)}, bf16[1,512,384]{2,1,0:T(8,128)(2,1)}, u32[]{:S(2)}) copy-start(bf16[1,512,384]{2,1,0:T(8,128)(2,1)} %param.10) | copy-start | bytes 1179652
  5.4 49.0 %all-to-all-start = ((bf16[64,8,1152]{2,1,0:T(8,128)(2,1)}), bf16[64,8,1152]{2,1,0:T(8,128)(2,1)S(1)}, u32[]{:S(2)}, u32[]{:S(2)}) async-start(bf16[64,8,1152]{2,1,0:T(8,128)(2,1)} %bitcast.3), calls=%async_computation | async-start | bytes 2359296 | tf_op jit(solution)/shard_map/all_to_all | solution.py:222
  25.3 3.3 %copy-start.3 = (bf16[512,128]{1,0:T(8,128)(2,1)}, bf16[512,128]{1,0:T(8,128)(2,1)S(1)}, u32[]{:S(2)}) copy-start(bf16[512,128]{1,0:T(8,128)(2,1)S(1)} %broadcast_in_dim.85.k_mask_ref) | copy-start | bytes 393220
  25.3 3.2 %copy-start.5 = (bf16[512,128]{1,0:T(8,128)(2,1)}, bf16[512,128]{1,0:T(8,128)(2,1)S(1)}, u32[]{:S(2)}) copy-start(bf16[512,128]{1,0:T(8,128)(2,1)S(1)} %broadcast_in_dim.80.q_mask_ref) | copy-start | bytes 393220
  91.0 1.0 copy-start.2
  92.0 7.1 %copy-start.1 = (bf16[1,512,384]{2,1,0:T(8,128)(2,1)S(1)}, bf16[1,512,384]{2,1,0:T(8,128)(2,1)}, u32[]{:S(2)}) copy-start(bf16[1,512,384]{2,1,0:T(8,128)(2,1)} %param.13) | copy-start | bytes 1179652
  92.0 38.6 %all-to-all-start.2 = ((bf16[64,8,1152]{2,1,0:T(8,128)(2,1)}), bf16[64,8,1152]{2,1,0:T(8,128)(2,1)S(1)}, u32[]{:S(2)}, u32[]{:S(2)}) async-start(bf16[64,8,1152]{2,1,0:T(8,128)(2,1)} %bitcast.30), calls=%async_computation.2 | async-start | bytes 2359296 | tf_op jit(solution)/shard_map/all_to_all | solution.py:222
  110.2 0.9 copy-start.4
  110.2 1.0 copy-start.6
  110.2 1.1 copy-start.10
  110.2 1.2 copy-start.12
  110.2 1.3 %copy-start.14 = (bf16[1,512,384]{2,1,0:T(8,128)(2,1)S(1)}, bf16[1,512,384]{2,1,0:T(8,128)(2,1)}, u32[]{:S(2)}) copy-start(bf16[1,512,384]{2,1,0:T(8,128)(2,1)} %param.10) | copy-start | bytes 1179652

commit v3 on v2

--- a/solution.py
+++ b/solution.py
@@ -13,6 +13,8 @@
 BF16 = jnp.bfloat16
 VMEM_BYTES = 24 * 1024 * 1024
 LOWEST = -3e38
+Z_PLACES = (6, 2, 0, 4, 7, 3, 1, 5)
+Y_PLACES = (4, 5, 6, 7, 0, 1, 2, 3)
 
 
 def dot(a, b, ca, cb):
@@ -82,15 +84,13 @@
 
 
 def time_value_kernel(
-    moved_ref, normed_ref, q_mask_ref, k_mask_ref, live_ref, out_ref, shift_ref, held, sem
+    moved_ref, normed_ref, q_mask_ref, k_mask_ref, live_ref, out_ref, shift_ref
 ):
     scale = HD ** (-0.5) * LOG2E
     width = normed_ref.shape[1]
-    heads = width // HD
-    copies = [pltpu.make_async_copy(normed_ref, out_ref.at[:, pl.ds(0, width)], sem.at[heads])]
-    copies[0].start()
+    out_ref[:, :width] = normed_ref[...]
     q_mask, k_mask, live = q_mask_ref[...], k_mask_ref[...], live_ref[...]
-    for h in range(heads):
+    for h in range(width // HD):
         q, k, g = (
             moved_ref[:, j * width + h * HD : j * width + (h + 1) * HD] for j in range(3)
         )
@@ -104,15 +104,7 @@
         shift_ref[h : h + 1, :] = jnp.where(
             live > 0, jnp.log2(inverse) - highest * scale, LOWEST
         )
-        held[h] = dot(weights, g, 1, 0).astype(BF16)
-        copies.append(
-            pltpu.make_async_copy(
-                held.at[h], out_ref.at[:, pl.ds(width + h * HD, HD)], sem.at[h]
-            )
-        )
-        copies[-1].start()
-    for copy in copies:
-        copy.wait()
+        out_ref[:, width + h * HD : width + (h + 1) * HD] = dot(weights, g, 1, 0).astype(BF16)
 
 
 def time_rest_kernel(
@@ -174,7 +166,6 @@
     full_channels = channels * lax.axis_size("head")
     positions_here = rows // lax.axis_size("frame")
     here = lax.axis_index("frame")
-    side = 8
 
     def head_block(width=1):
         return pl.BlockSpec((rows, width * HD), lambda h: (0, h))
@@ -210,11 +201,21 @@
             ),
         )
 
-    order = [z * side + y for y in range(side) for z in range(side)]
-    block_here = lax.rem(here, side) * side + lax.div(here, side)
+    def here_in(space, *arrays):
+        return [pltpu.with_memory_space_constraint(array, space) for array in arrays]
+
+    side = 8
+    order = [z * side + y for y in Y_PLACES for z in Z_PLACES]
+    numbers = jnp.arange(frames, dtype=jnp.int32)
+    order_row = sum(
+        jnp.where(numbers // side == i, y, 0) + jnp.where(numbers % side == i, side * z, 0)
+        for i, (y, z) in enumerate(zip(Y_PLACES, Z_PLACES))
+    )
+    block_here = jnp.sum(jnp.where(order_row == here, numbers, 0))
 
     def ordered(per_frame):
-        return per_frame.reshape(side, side).T.reshape(frames)
+        picked = order_row[:, None] == numbers[None, :]
+        return jnp.sum(jnp.where(picked, per_frame[None, :], 0), axis=1)
 
     def exchange(array):
         width = array.shape[-1]
@@ -236,10 +237,10 @@
         pack_kernel,
         [hbm] * 3,
         hbm,
-        jax.ShapeDtypeStruct((rows, 3 * channels), BF16),
+        pltpu.HBM((rows, 3 * channels), BF16),
         [pltpu.VMEM((3, rows, channels), BF16), dma((3,)), dma((3,))],
         traffic=6 * size,
-    )(query_time[0], key_time[0], cotangent[0])
+    )(*here_in(pltpu.HBM, query_time[0], key_time[0], cotangent[0]))
     moved = exchange(packed)
 
     clip_match = slot_clip[:, None] == jnp.arange(clip_res.shape[0], dtype=jnp.int32)[None, :]
@@ -276,25 +277,22 @@
     pair, shift = local(
         time_value_kernel,
         [vmem] * 5,
-        [hbm, vmem],
-        [
-            jax.ShapeDtypeStruct((rows, 2 * channels), BF16),
-            jax.ShapeDtypeStruct((8, rows), F32),
-        ],
-        [pltpu.VMEM((head_count, rows, HD), BF16), dma((head_count + 1,))],
+        [vmem, vmem],
+        [pltpu.VMEM((rows, 2 * channels), BF16), pltpu.VMEM((8, rows), F32)],
+        [],
         flops=3 * product,
         traffic=6 * size,
-    )(moved, normed, time_q_mask, time_k_mask, live_row)
+    )(*here_in(pltpu.VMEM, moved, normed, time_q_mask, time_k_mask, live_row))
     pair_moved = exchange(pair)
     results = local(
         time_rest_kernel,
         [vmem] * 5,
         hbm,
-        jax.ShapeDtypeStruct((rows, 3 * channels), BF16),
+        pltpu.HBM((rows, 3 * channels), BF16),
         [pltpu.VMEM((3, head_count, rows, HD), BF16), dma((3, head_count))],
         flops=6 * product,
         traffic=8 * size,
-    )(moved, pair_moved, time_q_mask, time_k_mask, shift)
+    )(*here_in(pltpu.VMEM, moved, pair_moved, time_q_mask, time_k_mask, shift))
     back = exchange(results)
 
     grad_value_back = pair_moved[:, channels:]
@@ -317,10 +315,10 @@
         finish_kernel,
         [vmem] * 2,
         [hbm] * 3,
-        [whole] * 3,
+        [pltpu.HBM((rows, channels), BF16)] * 3,
         [pltpu.VMEM((rows, channels), BF16), dma((3,))],
         traffic=7 * size,
-    )(back, normed)
+    )(*here_in(pltpu.VMEM, back, normed))
     return (
         mixed[None],
         grad_query_space[None],

time: 133 us -> 124 us (0.932)
  waiting for transfers between devices: 28.6 us -> 16.8 us
  starting transfers between devices: 23.2 us -> 30.5 us
  local copies, waits for them, and re-layouts: 6.54 us -> 1.08 us
  other arithmetic: 3.59 us -> 6.5 us
    all_to_all x2, waiting for transfers between devices: 28.6 us -> 16.8 us  [exchange(): lax.all_to_all(blocks, 'frame', split_axis=0, concat_axis=0, tiled=True,...]
    all_to_all x2, starting transfers between devices: 23.2 us -> 30.5 us  [exchange(): lax.all_to_all(blocks, 'frame', split_axis=0, concat_axis=0, tiled=True,...]
    unnamed x34 -> x20, local copies, waits for them, and re-layouts: 5.05 us -> 0.06 us
  transfers between devices with their start and end apart: 2 -> 2, of which waited for: 2 -> 2; matrix products, arithmetic and copies ran while one was open for 4% -> 6% of each run, Pallas kernels for 6% -> 7%
where the time goes in v3:
time: 124 us
  blocking collectives  50.9 us (41%)
  starting transfers between devices  30.5 us (25%)
  waiting for transfers between devices  16.8 us (14%)
  Pallas kernels  16.4 us (13%)
  other arithmetic  6.5 us (5%)
  between operations  1.6 us (1%)
    all_to_all x2, starting transfers between devices, exchange(): lax.all_to_all(blocks, 'frame', split_axis=0, concat_axis=0, tiled=True,...  30.5 us
    all_to_all x1, blocking collectives, exchange(): lax.all_to_all(blocks, 'frame', split_axis=0, concat_axis=0, tiled=True,...  29.6 us
    all_to_all x2, waiting for transfers between devices, exchange(): lax.all_to_all(blocks, 'frame', split_axis=0, concat_axis=0, tiled=True,...  16.8 us
    psum x1, blocking collectives, per_device(): square_sum = lax.psum(jnp.sum(space_out * space_out, axis=-1), 'head')  10.7 us
    psum x1, blocking collectives, per_device(): inner_norm = lax.psum(jnp.sum(grad_norm * normed_full, axis=-1), 'head')  10.6 us
    pallas_call x1, Pallas kernels, per_device(): call(space_backward_kernel, [head_block()] * 4 + [mask_spec, mask_spec],...  4.9 us
    pallas_call x1, Pallas kernels, per_device(): local(time_rest_kernel, [vmem] * 5, hbm, pltpu.HBM((rows, 3 * channels),...  3.55 us
    pallas_call x1, Pallas kernels, per_device(): call(space_forward_kernel, [head_block()] * 3 + [mask_spec, mask_spec, sh...  3.19 us
  transfers between devices with their start and end apart: 2, of which 2 were waited for; matrix products, arithmetic and copies ran while one was open for 6% of the time, Pallas kernels for 7%

profile of v3, /device:TPU:6, one launch (start us, length us, event | category | flops | bytes accessed | tf_op | source)
XLA Modules:
  0.0 123.8 jit_solution(2476718428132395985)
XLA Ops:
  0.6 2.1 %shard_map.127 = bf16[512,1152]{1,0:T(8,128)(2,1)} custom-call(bf16[512,384]{1,0:T(8,128)(2,1)} %bitcast.37, bf16[512,384]{1,0:T(8,128)(2,1)} %bitcast.38, bf16[512,384]{1,0:T(8,128)(2,1)} %bitcast.35), custom_call_target="tpu_custom_call" | custom-call | bytes 2359296 | tf_op jit(solution)/shard_map/pallas_call | solution.py:236
  2.8 0.0 copy-start.8
  2.8 0.0 copy-start.9
  2.8 0.0 copy-start
  2.8 0.0 copy-start.2
  2.8 0.0 copy-start.4
  2.8 18.8 %all-to-all-start = ((bf16[64,8,1152]{2,1,0:T(8,128)(2,1)}), bf16[64,8,1152]{2,1,0:T(8,128)(2,1)S(1)}, u32[]{:S(2)}, u32[]{:S(2)}) async-start(bf16[64,8,1152]{2,1,0:T(8,128)(2,1)} %bitcast.34), calls=%async_computation | async-start | bytes 2359296 | tf_op jit(solution)/shard_map/all_to_all | solution.py:223
  21.6 0.0 copy-done.8
  21.6 0.0 copy-done.9
  21.6 0.1 select_reduce_fusion.2
  21.7 0.6 dynamic_slice.3
  22.3 0.2 select_reduce_fusion
  22.5 0.1 iota_add_fusion
  22.6 0.1 add.245
  22.7 0.6 fusion.16
  24.0 0.1 fusion.17
  24.1 0.1 reshape.195.live_ref
  24.2 0.1 lt.93
  24.3 0.7 select_convert_fusion.1
  24.9 0.7 fusion.2.live_ref
  25.6 0.1 broadcast_in_dim.165.k_mask_ref
  25.8 0.0 copy-done
  25.8 0.0 copy-done.2
  25.8 0.0 copy-done.4
  25.8 3.2 %shard_map.128 = f32[512,384]{1,0:T(8,128)S(1)} custom-call(bf16[512,384]{1,0:T(8,128)(2,1)S(1)} %bitcast.28, bf16[512,384]{1,0:T(8,128)(2,1)S(1)} %bitcast.30, bf16[512,384]{1,0:T(8,128)(2,1)S(1)} %bitcast.32, bf16[512,128]{1,0:T(8,128)(2,1)S(1)} %broadcast_in_dim.160.q_mask_ref, bf16[512,128]{1,0:T(8,128)(2,1)S(1)} %broadcast_in_dim.165.k_mask_ref, ...), custom_call_target="tpu_custom_call" | custom-call | flops 603979776 | bytes 1966080 | tf_op jit(solution)/shard_map/pallas_call | solution.py:264
  29.0 0.1 multiply_reduce_fusion.1
  29.2 10.7 %psum.14 = f32[512]{0:T(512)S(1)} all-reduce(f32[512]{0:T(512)S(1)} %multiply_reduce_fusion.1), channel_id=1, replica_groups=mesh['frame'=64,'head'=8] {'head'}, use_global_device_ids=true, to_apply=%region_2.3 | all-reduce | flops 512 | bytes 4096 | tf_op jit(solution)/shard_map/psum | solution.py:272
  39.9 0.1 fusion.1.q_mask_ref
  40.0 0.2 select_convert_fusion.k_mask_ref
  40.2 0.0 copy-start.6
  40.3 0.1 multiply_convert_fusion.1.normed_ref
  40.4 9.3 %all-to-all-done = bf16[64,8,1152]{2,1,0:T(8,128)(2,1)S(1)} async-done(((bf16[64,8,1152]{2,1,0:T(8,128)(2,1)}), bf16[64,8,1152]{2,1,0:T(8,128)(2,1)S(1)}, u32[]{:S(2)}, u32[]{:S(2)}) %all-to-all-start) | async-done | bytes 1179680 | tf_op jit(solution)/shard_map/all_to_all | solution.py:223
  49.7 1.6 %shard_map.129 = (bf16[512,768]{1,0:T(8,128)(2,1)S(1)}, f32[8,512]{1,0:T(8,128)S(1)}) custom-call(bf16[512,1152]{1,0:T(8,128)(2,1)S(1)} %bitcast.25, bf16[512,384]{1,0:T(8,128)(2,1)S(1)} %multiply_convert_fusion.1.normed_ref, bf16[512,128]{1,0:T(8,128)(2,1)S(1)} %fusion.1.q_mask_ref, bf16[512,128]{1,0:T(8,128)(2,1)S(1)} %select_convert_fusion.k_mask_ref, ...), custom_call_target="tpu_custom_call" | custom-call | flops 603979776 | bytes 2359296 | tf_op jit(solution)/shard_map/pallas_call | solution.py:277
  51.3 0.0 copy-done.6
  51.4 0.0 copy-start.7
  51.4 29.6 %all_to_all.15 = bf16[64,8,768]{2,1,0:T(8,128)(2,1)S(1)} all-to-all(bf16[64,8,768]{2,1,0:T(8,128)(2,1)S(1)} %bitcast.27), channel_id=1, replica_groups={{416,160,32,288,480,224,96,352,424,168,40,296,488,232,104,360,432,176,4..., dimensions={0} | all-to-all | bytes 1572864 | tf_op jit(solution)/shard_map/all_to_all | solution.py:223
  81.0 0.0 copy-done.7
  81.0 3.5 %shard_map.130 = bf16[512,1152]{1,0:T(8,128)(2,1)} custom-call(bf16[512,1152]{1,0:T(8,128)(2,1)S(1)} %bitcast.26, bf16[512,768]{1,0:T(8,128)(2,1)S(1)} %bitcast.22, bf16[512,128]{1,0:T(8,128)(2,1)S(1)} %fusion.1.q_mask_ref, bf16[512,128]{1,0:T(8,128)(2,1)S(1)} %copy-done.7, f32[8,512]{1,0:T(8,128)S(1)} %get-tuple-element.15.shift_ref), custom_call_target="tpu_custom_call" | custom-call | flops 1207959552 | bytes 3145728 | tf_op jit(solution)/shard_map/pallas_call | solution.py:287
  84.6 11.7 %all-to-all-start.2 = ((bf16[64,8,1152]{2,1,0:T(8,128)(2,1)}), bf16[64,8,1152]{2,1,0:T(8,128)(2,1)S(1)}, u32[]{:S(2)}, u32[]{:S(2)}) async-start(bf16[64,8,1152]{2,1,0:T(8,128)(2,1)} %bitcast.36), calls=%async_computation.2 | async-start | bytes 2359296 | tf_op jit(solution)/shard_map/all_to_all | solution.py:223
  96.3 0.7 iota_compare_fusion.4
  97.0 1.4 %multiply_reduce_fusion = f32[512]{0:T(512)S(1)} fusion(f32[512,384]{1,0:T(8,128)S(1)} %shard_map.128, f32[512]{0:T(512)S(1)} %add_rsqrt_fusion, bf16[512,768]{1,0:T(8,128)(2,1)S(1)} %bitcast.23, pred[512]{0:T(512)(128)(4,1)S(1)} %iota_compare_fusion.4, bf16[1,512,384]{2,1,0:T(8,128)(2,1)} %param.13), kind=kLoop, calls=%fused_computation.1 | loop fusion | flops 1375744 | bytes 1577472 | tf_op jit(solution)/shard_map/reduce_sum | solution.py:301
  98.4 10.6 %psum.15 = f32[512]{0:T(512)S(1)} all-reduce(f32[512]{0:T(512)S(1)} %multiply_reduce_fusion), channel_id=1, replica_groups=mesh['frame'=64,'head'=8] {'head'}, use_global_device_ids=true, to_apply=%region_7.8 | all-reduce | flops 512 | bytes 4096 | tf_op jit(solution)/shard_map/psum | solution.py:301
  109.0 0.0 copy-start.1
  109.0 0.0 copy-start.3
  109.0 0.0 copy-start.5
  109.0 1.4 %multiply_convert_fusion.g_ref = bf16[512,384]{1,0:T(8,128)(2,1)S(1)} fusion(f32[512,384]{1,0:T(8,128)S(1)} %shard_map.128, f32[512]{0:T(512)S(1)} %broadcast_multiply_fusion, f32[512]{0:T(512)S(1)} %add_rsqrt_fusion, bf16[512,768]{1,0:T(8,128)(2,1)S(1)} %bitcast.24, pred[512]{0:T(512)(128)(4,1)S(1)} %iota_compare_fusion.4, bf16[1,512,384]{2,1,0:T(8,128)(2,1)} %param.13), kind=kLoop, calls=%fused_computation | loop fusion | flops 1769472 | bytes 1970688 | tf_op jit(solution)/shard_map/convert_element_type | solution.py:304
  110.4 0.0 copy-done.1
  110.4 0.0 copy-done.3
  110.4 0.0 copy-done.5
  110.4 4.9 %shard_map.132 = (bf16[512,384]{1,0:T(8,128)(2,1)}, bf16[512,384]{1,0:T(8,128)(2,1)}, bf16[512,384]{1,0:T(8,128)(2,1)}) custom-call(bf16[512,384]{1,0:T(8,128)(2,1)S(1)} %bitcast.29, bf16[512,384]{1,0:T(8,128)(2,1)S(1)} %bitcast.31, bf16[512,384]{1,0:T(8,128)(2,1)S(1)} %bitcast.33, bf16[512,384]{1,0:T(8,128)(2,1)S(1)} %multiply_convert_fusion.g_ref, ...), custom_call_target="tpu_custom_call" | custom-call | flops 1207959552 | bytes 2752512 | tf_op jit(solution)/shard_map/pallas_call | solution.py:305
  115.3 7.5 %all-to-all-done.2 = bf16[64,8,1152]{2,1,0:T(8,128)(2,1)S(1)} async-done(((bf16[64,8,1152]{2,1,0:T(8,128)(2,1)}), bf16[64,8,1152]{2,1,0:T(8,128)(2,1)S(1)}, u32[]{:S(2)}, u32[]{:S(2)}) %all-to-all-start.2) | async-done | bytes 1179680 | tf_op jit(solution)/shard_map/all_to_all | solution.py:223
  122.8 1.0 shard_map.131
  (7 shorter events, 0.1 us)
Async XLA Ops:
  2.8 18.8 %copy-start.8 = (s32[64]{0:T(128)S(1)}, s32[64]{0:T(128)}, u32[]{:S(2)}) copy-start(s32[64]{0:T(128)} %param.14) | copy-start | bytes 772
  2.8 18.8 %copy-start.9 = (s32[6]{0:T(128)S(1)}, s32[6]{0:T(128)}, u32[]{:S(2)}) copy-start(s32[6]{0:T(128)} %param.15) | copy-start | bytes 76
  2.8 23.0 %copy-start = (bf16[1,512,384]{2,1,0:T(8,128)(2,1)S(1)}, bf16[1,512,384]{2,1,0:T(8,128)(2,1)}, u32[]{:S(2)}) copy-start(bf16[1,512,384]{2,1,0:T(8,128)(2,1)} %param.8) | copy-start | bytes 1179652
  2.8 23.0 %copy-start.2 = (bf16[1,512,384]{2,1,0:T(8,128)(2,1)S(1)}, bf16[1,512,384]{2,1,0:T(8,128)(2,1)}, u32[]{:S(2)}) copy-start(bf16[1,512,384]{2,1,0:T(8,128)(2,1)} %param.9) | copy-start | bytes 1179652
  2.8 23.0 %copy-start.4 = (bf16[1,512,384]{2,1,0:T(8,128)(2,1)S(1)}, bf16[1,512,384]{2,1,0:T(8,128)(2,1)}, u32[]{:S(2)}) copy-start(bf16[1,512,384]{2,1,0:T(8,128)(2,1)} %param.10) | copy-start | bytes 1179652
  2.8 46.9 %all-to-all-start = ((bf16[64,8,1152]{2,1,0:T(8,128)(2,1)}), bf16[64,8,1152]{2,1,0:T(8,128)(2,1)S(1)}, u32[]{:S(2)}, u32[]{:S(2)}) async-start(bf16[64,8,1152]{2,1,0:T(8,128)(2,1)} %bitcast.34), calls=%async_computation | async-start | bytes 2359296 | tf_op jit(solution)/shard_map/all_to_all | solution.py:223
  40.2 11.1 %copy-start.6 = (bf16[512,128]{1,0:T(8,128)(2,1)}, bf16[512,128]{1,0:T(8,128)(2,1)S(1)}, u32[]{:S(2)}) copy-start(bf16[512,128]{1,0:T(8,128)(2,1)S(1)} %select_convert_fusion.k_mask_ref) | copy-start | bytes 393220
  51.4 29.7 %copy-start.7 = (bf16[512,128]{1,0:T(8,128)(2,1)S(1)}, bf16[512,128]{1,0:T(8,128)(2,1)}, u32[]{:S(2)}) copy-start(bf16[512,128]{1,0:T(8,128)(2,1)} %copy-done.6) | copy-start | bytes 393220
  84.6 38.2 %all-to-all-start.2 = ((bf16[64,8,1152]{2,1,0:T(8,128)(2,1)}), bf16[64,8,1152]{2,1,0:T(8,128)(2,1)S(1)}, u32[]{:S(2)}, u32[]{:S(2)}) async-start(bf16[64,8,1152]{2,1,0:T(8,128)(2,1)} %bitcast.36), calls=%async_computation.2 | async-start | bytes 2359296 | tf_op jit(solution)/shard_map/all_to_all | solution.py:223
  109.0 1.4 %copy-start.1 = (bf16[1,512,384]{2,1,0:T(8,128)(2,1)S(1)}, bf16[1,512,384]{2,1,0:T(8,128)(2,1)}, u32[]{:S(2)}) copy-start(bf16[1,512,384]{2,1,0:T(8,128)(2,1)} %param.8) | copy-start | bytes 1179652
  109.0 1.5 %copy-start.3 = (bf16[1,512,384]{2,1,0:T(8,128)(2,1)S(1)}, bf16[1,512,384]{2,1,0:T(8,128)(2,1)}, u32[]{:S(2)}) copy-start(bf16[1,512,384]{2,1,0:T(8,128)(2,1)} %param.9) | copy-start | bytes 1179652
  109.0 1.5 %copy-start.5 = (bf16[1,512,384]{2,1,0:T(8,128)(2,1)S(1)}, bf16[1,512,384]{2,1,0:T(8,128)(2,1)}, u32[]{:S(2)}) copy-start(bf16[1,512,384]{2,1,0:T(8,128)(2,1)} %param.10) | copy-start | bytes 1179652

commit v4 on v3

--- a/solution.py
+++ b/solution.py
@@ -13,7 +13,7 @@
 BF16 = jnp.bfloat16
 VMEM_BYTES = 24 * 1024 * 1024
 LOWEST = -3e38
-Z_PLACES = (6, 2, 0, 4, 7, 3, 1, 5)
+Z_PLACES = (4, 5, 6, 7, 0, 1, 2, 3)
 Y_PLACES = (4, 5, 6, 7, 0, 1, 2, 3)
 
 
@@ -112,32 +112,44 @@
 ):
     scale = HD ** (-0.5)
     width = pair_ref.shape[1] // 2
-    heads = width // HD
+    heads = range(width // HD)
     copies = []
     q_mask, k_mask = q_mask_ref[...], k_mask_ref[...]
-    for h in range(heads):
-        q, k, g = (
-            moved_ref[:, j * width + h * HD : j * width + (h + 1) * HD] for j in range(3)
-        )
-        v = pair_ref[:, h * HD : (h + 1) * HD]
+
+    def moved(j, h):
+        return moved_ref[:, j * width + h * HD : j * width + (h + 1) * HD]
+
+    def values(h):
+        return pair_ref[:, h * HD : (h + 1) * HD]
+
+    def send(j, h, result):
+        held[j, h] = result.astype(BF16)
+        copies.append(
+            pltpu.make_async_copy(
+                held.at[j, h], out_ref.at[:, pl.ds(j * width + h * HD, HD)], sem.at[j, h]
+            )
+        )
+        copies[-1].start()
+
+    weights = []
+    for h in heads:
         scores = dot(
-            jnp.concatenate([k, k_mask], axis=1), jnp.concatenate([q, q_mask], axis=1), 1, 1
-        )
-        weights = jnp.exp2(scores * (scale * LOG2E) + shift_ref[h : h + 1, :])
-        time_out = dot(weights.astype(BF16), v, 0, 0)
-        grad_weights = dot(v, g, 1, 1)
-        inner = jnp.sum(weights * grad_weights, axis=0, keepdims=True)
-        grad_scores = (weights * (grad_weights - inner)).astype(BF16)
-        grad_query = dot(grad_scores, k, 0, 0) * scale
-        grad_key = dot(grad_scores, q, 1, 0) * scale
-        for j, result in enumerate((time_out, grad_query, grad_key)):
-            held[j, h] = result.astype(BF16)
-            copies.append(
-                pltpu.make_async_copy(
-                    held.at[j, h], out_ref.at[:, pl.ds(j * width + h * HD, HD)], sem.at[j, h]
-                )
-            )
-            copies[-1].start()
+            jnp.concatenate([moved(1, h), k_mask], axis=1),
+            jnp.concatenate([moved(0, h), q_mask], axis=1),
+            1,
+            1,
+        )
+        weights.append(jnp.exp2(scores * (scale * LOG2E) + shift_ref[h : h + 1, :]))
+    grad_weights = [dot(values(h), moved(2, h), 1, 1) for h in heads]
+    for h in heads:
+        send(0, h, dot(weights[h].astype(BF16), values(h), 0, 0))
+    grad_scores = []
+    for h in heads:
+        inner = jnp.sum(weights[h] * grad_weights[h], axis=0, keepdims=True)
+        grad_scores.append((weights[h] * (grad_weights[h] - inner)).astype(BF16))
+    for h in heads:
+        send(1, h, dot(grad_scores[h], moved(1, h), 0, 0) * scale)
+        send(2, h, dot(grad_scores[h], moved(0, h), 1, 0) * scale)
     for copy in copies:
         copy.wait()
 
@@ -205,10 +217,10 @@
         return [pltpu.with_memory_space_constraint(array, space) for array in arrays]
 
     side = 8
-    order = [z * side + y for y in Y_PLACES for z in Z_PLACES]
+    order = [z * side + y for z in Z_PLACES for y in Y_PLACES]
     numbers = jnp.arange(frames, dtype=jnp.int32)
     order_row = sum(
-        jnp.where(numbers // side == i, y, 0) + jnp.where(numbers % side == i, side * z, 0)
+        jnp.where(numbers // side == i, side * z, 0) + jnp.where(numbers % side == i, y, 0)
         for i, (y, z) in enumerate(zip(Y_PLACES, Z_PLACES))
     )
     block_here = jnp.sum(jnp.where(order_row == here, numbers, 0))

time: 124 us -> 123 us (level)
  waiting for transfers between devices: 16.8 us -> 13.3 us
  starting transfers between devices: 30.5 us -> 33 us
    all_to_all x2, waiting for transfers between devices: 16.8 us -> 13.3 us  [exchange(): lax.all_to_all(blocks, 'frame', split_axis=0, concat_axis=0, tiled=True,...]
    all_to_all x2, starting transfers between devices: 30.5 us -> 33 us  [exchange(): lax.all_to_all(blocks, 'frame', split_axis=0, concat_axis=0, tiled=True,...]
where the time goes in v4:
time: 123 us; the launch traced here: 122 us
  blocking collectives  50.5 us (41%)
  starting transfers between devices  33 us (27%)
  Pallas kernels  16.2 us (13%)
  waiting for transfers between devices  13.3 us (11%)
  other arithmetic  6.5 us (5%)
  between operations  1.6 us (1%)
    all_to_all x2, starting transfers between devices, exchange(): lax.all_to_all(blocks, 'frame', split_axis=0, concat_axis=0, tiled=True,...  33 us
    all_to_all x1, blocking collectives, exchange(): lax.all_to_all(blocks, 'frame', split_axis=0, concat_axis=0, tiled=True,...  29.3 us
    all_to_all x2, waiting for transfers between devices, exchange(): lax.all_to_all(blocks, 'frame', split_axis=0, concat_axis=0, tiled=True,...  13.3 us
    psum x1, blocking collectives, per_device(): square_sum = lax.psum(jnp.sum(space_out * space_out, axis=-1), 'head')  10.6 us
    psum x1, blocking collectives, per_device(): inner_norm = lax.psum(jnp.sum(grad_norm * normed_full, axis=-1), 'head')  10.6 us
    pallas_call x1, Pallas kernels, per_device(): call(space_backward_kernel, [head_block()] * 4 + [mask_spec, mask_spec],...  4.9 us
    pallas_call x1, Pallas kernels, per_device(): local(time_rest_kernel, [vmem] * 5, hbm, pltpu.HBM((rows, 3 * channels),...  3.32 us
    pallas_call x1, Pallas kernels, per_device(): call(space_forward_kernel, [head_block()] * 3 + [mask_spec, mask_spec, sh...  3.19 us
  transfers between devices with their start and end apart: 2, of which 2 were waited for; matrix products, arithmetic and copies ran while one was open for 6% of the time, Pallas kernels for 7%

profile of v4, /device:TPU:6, one launch (start us, length us, event | category | flops | bytes accessed | tf_op | source)
XLA Modules:
  0.0 122.2 jit_solution(13406297216798052717)
XLA Ops:
  0.6 2.1 %shard_map.127 = bf16[512,1152]{1,0:T(8,128)(2,1)} custom-call(bf16[512,384]{1,0:T(8,128)(2,1)} %bitcast.37, bf16[512,384]{1,0:T(8,128)(2,1)} %bitcast.38, bf16[512,384]{1,0:T(8,128)(2,1)} %bitcast.35), custom_call_target="tpu_custom_call" | custom-call | bytes 2359296 | tf_op jit(solution)/shard_map/pallas_call | solution.py:248
  2.8 0.0 copy-start.8
  2.8 0.0 copy-start.9
  2.8 0.0 copy-start
  2.8 0.0 copy-start.2
  2.8 0.0 copy-start.4
  2.8 20.0 %all-to-all-start = ((bf16[64,8,1152]{2,1,0:T(8,128)(2,1)}), bf16[64,8,1152]{2,1,0:T(8,128)(2,1)S(1)}, u32[]{:S(2)}, u32[]{:S(2)}) async-start(bf16[64,8,1152]{2,1,0:T(8,128)(2,1)} %bitcast.34), calls=%async_computation | async-start | bytes 2359296 | tf_op jit(solution)/shard_map/all_to_all | solution.py:235
  22.9 0.0 copy-done.8
  22.9 0.0 copy-done.9
  22.9 0.1 select_reduce_fusion.2
  23.0 0.6 dynamic_slice.3
  23.6 0.2 select_reduce_fusion
  23.8 0.1 iota_add_fusion
  23.8 0.1 add.245
  23.9 0.6 fusion.16
  25.2 0.1 fusion.17
  25.3 0.1 reshape.195.live_ref
  25.4 0.1 lt.93
  25.5 0.7 select_convert_fusion.1
  26.2 0.7 fusion.2.live_ref
  26.9 0.1 broadcast_in_dim.165.k_mask_ref
  27.0 0.0 copy-done
  27.0 0.0 copy-done.2
  27.1 0.0 copy-done.4
  27.1 3.2 %shard_map.128 = f32[512,384]{1,0:T(8,128)S(1)} custom-call(bf16[512,384]{1,0:T(8,128)(2,1)S(1)} %bitcast.28, bf16[512,384]{1,0:T(8,128)(2,1)S(1)} %bitcast.30, bf16[512,384]{1,0:T(8,128)(2,1)S(1)} %bitcast.32, bf16[512,128]{1,0:T(8,128)(2,1)S(1)} %broadcast_in_dim.160.q_mask_ref, bf16[512,128]{1,0:T(8,128)(2,1)S(1)} %broadcast_in_dim.165.k_mask_ref, ...), custom_call_target="tpu_custom_call" | custom-call | flops 603979776 | bytes 1966080 | tf_op jit(solution)/shard_map/pallas_call | solution.py:276
  30.3 0.1 multiply_reduce_fusion.1
  30.4 10.6 %psum.14 = f32[512]{0:T(512)S(1)} all-reduce(f32[512]{0:T(512)S(1)} %multiply_reduce_fusion.1), channel_id=1, replica_groups=mesh['frame'=64,'head'=8] {'head'}, use_global_device_ids=true, to_apply=%region_2.3 | all-reduce | flops 512 | bytes 4096 | tf_op jit(solution)/shard_map/psum | solution.py:284
  41.0 0.1 fusion.1.q_mask_ref
  41.2 0.2 select_convert_fusion.k_mask_ref
  41.4 0.0 copy-start.6
  41.4 0.1 multiply_convert_fusion.1.normed_ref
  41.5 7.6 %all-to-all-done = bf16[64,8,1152]{2,1,0:T(8,128)(2,1)S(1)} async-done(((bf16[64,8,1152]{2,1,0:T(8,128)(2,1)}), bf16[64,8,1152]{2,1,0:T(8,128)(2,1)S(1)}, u32[]{:S(2)}, u32[]{:S(2)}) %all-to-all-start) | async-done | bytes 1179680 | tf_op jit(solution)/shard_map/all_to_all | solution.py:235
  49.2 1.6 %shard_map.129 = (bf16[512,768]{1,0:T(8,128)(2,1)S(1)}, f32[8,512]{1,0:T(8,128)S(1)}) custom-call(bf16[512,1152]{1,0:T(8,128)(2,1)S(1)} %bitcast.25, bf16[512,384]{1,0:T(8,128)(2,1)S(1)} %multiply_convert_fusion.1.normed_ref, bf16[512,128]{1,0:T(8,128)(2,1)S(1)} %fusion.1.q_mask_ref, bf16[512,128]{1,0:T(8,128)(2,1)S(1)} %select_convert_fusion.k_mask_ref, ...), custom_call_target="tpu_custom_call" | custom-call | flops 603979776 | bytes 2359296 | tf_op jit(solution)/shard_map/pallas_call | solution.py:289
  50.8 0.0 copy-done.6
  50.8 0.0 copy-start.7
  50.8 29.3 %all_to_all.15 = bf16[64,8,768]{2,1,0:T(8,128)(2,1)S(1)} all-to-all(bf16[64,8,768]{2,1,0:T(8,128)(2,1)S(1)} %bitcast.27), channel_id=1, replica_groups={{288,296,304,312,256,264,272,280,352,360,368,376,320,328,336,344,416,42..., dimensions={0} | all-to-all | bytes 1572864 | tf_op jit(solution)/shard_map/all_to_all | solution.py:235
  80.1 0.0 copy-done.7
  80.1 3.3 %shard_map.130 = bf16[512,1152]{1,0:T(8,128)(2,1)} custom-call(bf16[512,1152]{1,0:T(8,128)(2,1)S(1)} %bitcast.26, bf16[512,768]{1,0:T(8,128)(2,1)S(1)} %bitcast.22, bf16[512,128]{1,0:T(8,128)(2,1)S(1)} %fusion.1.q_mask_ref, bf16[512,128]{1,0:T(8,128)(2,1)S(1)} %copy-done.7, f32[8,512]{1,0:T(8,128)S(1)} %get-tuple-element.15.shift_ref), custom_call_target="tpu_custom_call" | custom-call | flops 1207959552 | bytes 3145728 | tf_op jit(solution)/shard_map/pallas_call | solution.py:299
  83.5 13.0 %all-to-all-start.2 = ((bf16[64,8,1152]{2,1,0:T(8,128)(2,1)}), bf16[64,8,1152]{2,1,0:T(8,128)(2,1)S(1)}, u32[]{:S(2)}, u32[]{:S(2)}) async-start(bf16[64,8,1152]{2,1,0:T(8,128)(2,1)} %bitcast.36), calls=%async_computation.2 | async-start | bytes 2359296 | tf_op jit(solution)/shard_map/all_to_all | solution.py:235
  96.4 0.7 iota_compare_fusion.4
  97.1 1.4 %multiply_reduce_fusion = f32[512]{0:T(512)S(1)} fusion(f32[512,384]{1,0:T(8,128)S(1)} %shard_map.128, f32[512]{0:T(512)S(1)} %add_rsqrt_fusion, bf16[512,768]{1,0:T(8,128)(2,1)S(1)} %bitcast.23, pred[512]{0:T(512)(128)(4,1)S(1)} %iota_compare_fusion.4, bf16[1,512,384]{2,1,0:T(8,128)(2,1)} %param.13), kind=kLoop, calls=%fused_computation.1 | loop fusion | flops 1375744 | bytes 1577472 | tf_op jit(solution)/shard_map/reduce_sum | solution.py:313
  98.5 10.6 %psum.15 = f32[512]{0:T(512)S(1)} all-reduce(f32[512]{0:T(512)S(1)} %multiply_reduce_fusion), channel_id=1, replica_groups=mesh['frame'=64,'head'=8] {'head'}, use_global_device_ids=true, to_apply=%region_7.8 | all-reduce | flops 512 | bytes 4096 | tf_op jit(solution)/shard_map/psum | solution.py:313
  109.1 0.0 copy-start.1
  109.1 0.0 copy-start.3
  109.1 0.0 copy-start.5
  109.1 1.4 %multiply_convert_fusion.g_ref = bf16[512,384]{1,0:T(8,128)(2,1)S(1)} fusion(f32[512,384]{1,0:T(8,128)S(1)} %shard_map.128, f32[512]{0:T(512)S(1)} %broadcast_multiply_fusion, f32[512]{0:T(512)S(1)} %add_rsqrt_fusion, bf16[512,768]{1,0:T(8,128)(2,1)S(1)} %bitcast.24, pred[512]{0:T(512)(128)(4,1)S(1)} %iota_compare_fusion.4, bf16[1,512,384]{2,1,0:T(8,128)(2,1)} %param.13), kind=kLoop, calls=%fused_computation | loop fusion | flops 1769472 | bytes 1970688 | tf_op jit(solution)/shard_map/convert_element_type | solution.py:316
  110.5 0.0 copy-done.1
  110.6 0.0 copy-done.3
  110.6 0.0 copy-done.5
  110.6 4.9 %shard_map.132 = (bf16[512,384]{1,0:T(8,128)(2,1)}, bf16[512,384]{1,0:T(8,128)(2,1)}, bf16[512,384]{1,0:T(8,128)(2,1)}) custom-call(bf16[512,384]{1,0:T(8,128)(2,1)S(1)} %bitcast.29, bf16[512,384]{1,0:T(8,128)(2,1)S(1)} %bitcast.31, bf16[512,384]{1,0:T(8,128)(2,1)S(1)} %bitcast.33, bf16[512,384]{1,0:T(8,128)(2,1)S(1)} %multiply_convert_fusion.g_ref, ...), custom_call_target="tpu_custom_call" | custom-call | flops 1207959552 | bytes 2752512 | tf_op jit(solution)/shard_map/pallas_call | solution.py:317
  115.5 5.7 %all-to-all-done.2 = bf16[64,8,1152]{2,1,0:T(8,128)(2,1)S(1)} async-done(((bf16[64,8,1152]{2,1,0:T(8,128)(2,1)}), bf16[64,8,1152]{2,1,0:T(8,128)(2,1)S(1)}, u32[]{:S(2)}, u32[]{:S(2)}) %all-to-all-start.2) | async-done | bytes 1179680 | tf_op jit(solution)/shard_map/all_to_all | solution.py:235
  121.2 1.0 shard_map.131
  (7 shorter events, 0.1 us)
Async XLA Ops:
  2.8 20.1 %copy-start.8 = (s32[64]{0:T(128)S(1)}, s32[64]{0:T(128)}, u32[]{:S(2)}) copy-start(s32[64]{0:T(128)} %param.14) | copy-start | bytes 772
  2.8 20.1 %copy-start.9 = (s32[6]{0:T(128)S(1)}, s32[6]{0:T(128)}, u32[]{:S(2)}) copy-start(s32[6]{0:T(128)} %param.15) | copy-start | bytes 76
  2.8 24.2 %copy-start = (bf16[1,512,384]{2,1,0:T(8,128)(2,1)S(1)}, bf16[1,512,384]{2,1,0:T(8,128)(2,1)}, u32[]{:S(2)}) copy-start(bf16[1,512,384]{2,1,0:T(8,128)(2,1)} %param.8) | copy-start | bytes 1179652
  2.8 24.2 %copy-start.2 = (bf16[1,512,384]{2,1,0:T(8,128)(2,1)S(1)}, bf16[1,512,384]{2,1,0:T(8,128)(2,1)}, u32[]{:S(2)}) copy-start(bf16[1,512,384]{2,1,0:T(8,128)(2,1)} %param.9) | copy-start | bytes 1179652
  2.8 24.2 %copy-start.4 = (bf16[1,512,384]{2,1,0:T(8,128)(2,1)S(1)}, bf16[1,512,384]{2,1,0:T(8,128)(2,1)}, u32[]{:S(2)}) copy-start(bf16[1,512,384]{2,1,0:T(8,128)(2,1)} %param.10) | copy-start | bytes 1179652
  2.8 46.3 %all-to-all-start = ((bf16[64,8,1152]{2,1,0:T(8,128)(2,1)}), bf16[64,8,1152]{2,1,0:T(8,128)(2,1)S(1)}, u32[]{:S(2)}, u32[]{:S(2)}) async-start(bf16[64,8,1152]{2,1,0:T(8,128)(2,1)} %bitcast.34), calls=%async_computation | async-start | bytes 2359296 | tf_op jit(solution)/shard_map/all_to_all | solution.py:235
  41.4 9.4 %copy-start.6 = (bf16[512,128]{1,0:T(8,128)(2,1)}, bf16[512,128]{1,0:T(8,128)(2,1)S(1)}, u32[]{:S(2)}) copy-start(bf16[512,128]{1,0:T(8,128)(2,1)S(1)} %select_convert_fusion.k_mask_ref) | copy-start | bytes 393220
  50.8 29.3 %copy-start.7 = (bf16[512,128]{1,0:T(8,128)(2,1)S(1)}, bf16[512,128]{1,0:T(8,128)(2,1)}, u32[]{:S(2)}) copy-start(bf16[512,128]{1,0:T(8,128)(2,1)} %copy-done.6) | copy-start | bytes 393220
  83.5 37.7 %all-to-all-start.2 = ((bf16[64,8,1152]{2,1,0:T(8,128)(2,1)}), bf16[64,8,1152]{2,1,0:T(8,128)(2,1)S(1)}, u32[]{:S(2)}, u32[]{:S(2)}) async-start(bf16[64,8,1152]{2,1,0:T(8,128)(2,1)} %bitcast.36), calls=%async_computation.2 | async-start | bytes 2359296 | tf_op jit(solution)/shard_map/all_to_all | solution.py:235
  109.1 1.4 %copy-start.1 = (bf16[1,512,384]{2,1,0:T(8,128)(2,1)S(1)}, bf16[1,512,384]{2,1,0:T(8,128)(2,1)}, u32[]{:S(2)}) copy-start(bf16[1,512,384]{2,1,0:T(8,128)(2,1)} %param.8) | copy-start | bytes 1179652
  109.1 1.5 %copy-start.3 = (bf16[1,512,384]{2,1,0:T(8,128)(2,1)S(1)}, bf16[1,512,384]{2,1,0:T(8,128)(2,1)}, u32[]{:S(2)}) copy-start(bf16[1,512,384]{2,1,0:T(8,128)(2,1)} %param.9) | copy-start | bytes 1179652
  109.1 1.5 %copy-start.5 = (bf16[1,512,384]{2,1,0:T(8,128)(2,1)S(1)}, bf16[1,512,384]{2,1,0:T(8,128)(2,1)}, u32[]{:S(2)}) copy-start(bf16[1,512,384]{2,1,0:T(8,128)(2,1)} %param.10) | copy-start | bytes 1179652

commit v5 on v4

--- a/solution.py
+++ b/solution.py
@@ -21,34 +21,69 @@
     return lax.dot_general(a, b, (((ca,), (cb,)), ((), ())), preferred_element_type=F32)
 
 
-def softmax_keys_first(q, k, q_mask, k_mask):
-    scale = HD ** (-0.5)
-    scores = dot(
-        jnp.concatenate([k, k_mask], axis=1), jnp.concatenate([q, q_mask], axis=1), 1, 1
-    )
-    highest = jnp.max(scores, axis=0, keepdims=True)
-    expanded = jnp.exp2((scores - highest) * (scale * LOG2E))
-    return expanded, 1.0 / jnp.sum(expanded, axis=0, keepdims=True)
-
-
-def softmax_queries_first(q, k, q_mask, k_mask):
-    scale = HD ** (-0.5)
-    scores = dot(
-        jnp.concatenate([q, q_mask], axis=1), jnp.concatenate([k, k_mask], axis=1), 1, 1
-    )
-    highest = jnp.max(scores, axis=1, keepdims=True)
-    expanded = jnp.exp2((scores - highest) * (scale * LOG2E))
-    return expanded, 1.0 / jnp.sum(expanded, axis=1, keepdims=True)
-
-
-def pack_kernel(a_ref, b_ref, c_ref, out_ref, held, in_sem, out_sem):
+def space_forward(
+    q_ref, k_ref, v_ref, clip_ref, res_ref, out_ref, weights_ref, held, kept,
+    clips, sizes, sem, core,
+):
+    @pl.when(lax.rem(lax.axis_index("head"), 2) == core)
+    def _():
+        copies = [
+            pltpu.make_async_copy(ref, held.at[i], sem.at[i])
+            for i, ref in enumerate((q_ref, k_ref, v_ref))
+        ]
+        small = [
+            pltpu.make_async_copy(clip_ref, clips, sem.at[3]),
+            pltpu.make_async_copy(res_ref, sizes, sem.at[4]),
+        ]
+        for copy in copies + small:
+            copy.start()
+        for copy in small:
+            copy.wait()
+        rows, width = out_ref.shape
+        live_count = sizes[clips[lax.axis_index("frame")]]
+        allowed = lax.broadcasted_iota(jnp.int32, (1, rows), 1) < live_count
+        live = (lax.broadcasted_iota(jnp.int32, (rows, 1), 0) < live_count).astype(F32)
+        scale = HD ** (-0.5) * LOG2E
+        for copy in copies:
+            copy.wait()
+        for h in range(width // HD):
+            q, k, v = (held[j, :, h * HD : (h + 1) * HD] for j in range(3))
+            scores = jnp.where(allowed, dot(q, k, 1, 1), NEGATIVE)
+            highest = jnp.max(scores, axis=1, keepdims=True)
+            expanded = jnp.exp2((scores - highest) * scale)
+            inverse = 1.0 / jnp.sum(expanded, axis=1, keepdims=True)
+            weights = (expanded * inverse).astype(BF16)
+            out_ref[:, h * HD : (h + 1) * HD] = dot(weights, v, 1, 0) * live
+        allowed = lax.broadcasted_iota(jnp.int32, (rows, 1), 0) < live_count
+        stores = []
+        for h in range(width // HD):
+            q, k = (held[j, :, h * HD : (h + 1) * HD] for j in range(2))
+            scores = jnp.where(allowed, dot(k, q, 1, 1), NEGATIVE)
+            highest = jnp.max(scores, axis=0, keepdims=True)
+            expanded = jnp.exp2((scores - highest) * scale)
+            inverse = 1.0 / jnp.sum(expanded, axis=0, keepdims=True)
+            kept[h] = expanded * inverse
+            stores.append(pltpu.make_async_copy(kept.at[h], weights_ref.at[h], sem.at[5 + h]))
+            stores[-1].start()
+        for store in stores:
+            store.wait()
+
+
+def pack_kernel(
+    q_ref, k_ref, v_ref, clip_ref, res_ref, a_ref, b_ref, c_ref, packed_ref, out_ref,
+    weights_ref, held, kept, clips, sizes, space_sem, in_sem, out_sem,
+):
+    space_forward(
+        q_ref, k_ref, v_ref, clip_ref, res_ref, out_ref, weights_ref, held, kept, clips, sizes,
+        space_sem, 0,
+    )
     width = a_ref.shape[1]
     loads, stores = [], []
     for i, ref in enumerate((a_ref, b_ref, c_ref)):
         loads.append(pltpu.make_async_copy(ref, held.at[i], in_sem.at[i]))
         stores.append(
             pltpu.make_async_copy(
-                held.at[i], out_ref.at[:, pl.ds(i * width, width)], out_sem.at[i]
+                held.at[i], packed_ref.at[:, pl.ds(i * width, width)], out_sem.at[i]
             )
         )
     for load in loads:
@@ -60,21 +95,20 @@
         store.wait()
 
 
-def space_forward_kernel(q_ref, k_ref, v_ref, q_mask_ref, k_mask_ref, live_ref, out_ref):
-    expanded, inverse = softmax_queries_first(
-        q_ref[...], k_ref[...], q_mask_ref[...], k_mask_ref[...]
-    )
-    weights = (expanded * inverse).astype(BF16)
-    out_ref[...] = dot(weights, v_ref[...], 1, 0) * live_ref[...]
-
-
-def space_backward_kernel(
-    q_ref, k_ref, v_ref, g_ref, q_mask_ref, k_mask_ref, gq_ref, gk_ref, gv_ref
-):
+def space_rest_kernel(
+    q_ref, k_ref, v_ref, clip_ref, res_ref, given_ref, given_weights_ref, out_ref, weights_ref,
+    held, kept, clips, sizes, sem,
+):
+    space_forward(
+        q_ref, k_ref, v_ref, clip_ref, res_ref, out_ref, weights_ref, held, kept, clips, sizes,
+        sem, 1,
+    )
+
+
+def space_backward_kernel(q_ref, k_ref, v_ref, g_ref, weights_ref, gq_ref, gk_ref, gv_ref):
     scale = HD ** (-0.5)
     q, k, v, g = q_ref[...], k_ref[...], v_ref[...], g_ref[...]
-    expanded, inverse = softmax_keys_first(q, k, q_mask_ref[...], k_mask_ref[...])
-    weights = expanded * inverse
+    weights = weights_ref[0]
     gv_ref[...] = dot(weights.astype(BF16), g, 1, 0).astype(BF16)
     grad_weights = dot(v, g, 1, 1)
     inner = jnp.sum(weights * grad_weights, axis=0, keepdims=True)
@@ -182,9 +216,6 @@
     def head_block(width=1):
         return pl.BlockSpec((rows, width * HD), lambda h: (0, h))
 
-    def shared(shape):
-        return pl.BlockSpec(shape, lambda h: (0,) * len(shape))
-
     def call(kernel, in_specs, out_specs, out_shape, flops=0, traffic=0):
         return pl.pallas_call(
             kernel,
@@ -200,13 +231,16 @@
             ),
         )
 
-    def local(kernel, in_specs, out_specs, out_shape, scratch, flops=0, traffic=0):
+    def local(
+        kernel, in_specs, out_specs, out_shape, scratch, flops=0, traffic=0, aliases={}
+    ):
         return pl.pallas_call(
             kernel,
             in_specs=in_specs,
             out_specs=out_specs,
             out_shape=out_shape,
             scratch_shapes=scratch,
+            input_output_aliases=aliases,
             compiler_params=pltpu.CompilerParams(vmem_limit_bytes=VMEM_BYTES),
             cost_estimate=pl.CostEstimate(
                 flops=flops, bytes_accessed=traffic, transcendentals=0
@@ -245,14 +279,22 @@
 
     hbm, vmem = pl.BlockSpec(memory_space=pltpu.HBM), pl.BlockSpec(memory_space=pltpu.VMEM)
     dma = pltpu.SemaphoreType.DMA
-    packed = local(
+    space = here_in(pltpu.HBM, q_space, k_space, v_space, slot_clip, clip_res)
+    scalars = [pltpu.SMEM((frames,), jnp.int32), pltpu.SMEM(clip_res.shape, jnp.int32)]
+    kept = [
+        pltpu.VMEM((rows, channels), F32),
+        pltpu.HBM((head_count, rows, rows), F32),
+    ]
+    weights_held = pltpu.VMEM((head_count, rows, rows), F32)
+    space_sems = dma((5 + head_count,))
+    packed, space_out, space_weights = local(
         pack_kernel,
-        [hbm] * 3,
-        hbm,
-        pltpu.HBM((rows, 3 * channels), BF16),
-        [pltpu.VMEM((3, rows, channels), BF16), dma((3,)), dma((3,))],
+        [hbm] * 8,
+        [hbm, vmem, hbm],
+        [pltpu.HBM((rows, 3 * channels), BF16)] + kept,
+        [pltpu.VMEM((3, rows, channels), BF16), weights_held, *scalars, space_sems, dma((3,)), dma((3,))],
         traffic=6 * size,
-    )(*here_in(pltpu.HBM, query_time[0], key_time[0], cotangent[0]))
+    )(*space, *here_in(pltpu.HBM, query_time[0], key_time[0], cotangent[0]))
     moved = exchange(packed)
 
     clip_match = slot_clip[:, None] == jnp.arange(clip_res.shape[0], dtype=jnp.int32)[None, :]
@@ -260,9 +302,6 @@
     local_res = lax.dynamic_slice_in_dim(slot_res, here, 1, 0)
     live_space = jnp.arange(rows, dtype=jnp.int32) < local_res
     column = jnp.arange(HD, dtype=jnp.int32)[None, :]
-    space_q_mask = jnp.broadcast_to(column == 0, (rows, HD)).astype(BF16)
-    space_k_mask = jnp.where(live_space[:, None], 0.0, NEGATIVE).astype(BF16)
-    space_k_mask = jnp.broadcast_to(space_k_mask, (rows, HD))
     place = jnp.arange(positions_here, dtype=jnp.int32)[None, :]
     live_time = (block_here * positions_here + place) < ordered(slot_res)[:, None]
     group = ordered(slot_clip)[:, None] * positions_here + place
@@ -272,15 +311,16 @@
     time_k_mask = time_k_mask.astype(BF16)
     live_row = live_time.reshape(1, rows).astype(F32)
 
-    mask_spec = shared((rows, HD))
-    space_out = call(
-        space_forward_kernel,
-        [head_block()] * 3 + [mask_spec, mask_spec, shared((rows, 1))],
-        head_block(),
-        jax.ShapeDtypeStruct((rows, channels), F32),
-        flops=3 * product,
+    space_out, space_weights = local(
+        space_rest_kernel,
+        [hbm] * 5 + [vmem, hbm],
+        [vmem, hbm],
+        kept,
+        [pltpu.VMEM((3, rows, channels), BF16), weights_held, *scalars, space_sems],
+        flops=2 * product,
         traffic=5 * size,
-    )(q_space, k_space, v_space, space_q_mask, space_k_mask, live_space[:, None].astype(F32))
+        aliases={5: 0, 6: 1},
+    )(*space, *here_in(pltpu.VMEM, space_out), *here_in(pltpu.HBM, space_weights))
     square_sum = lax.psum(jnp.sum(space_out * space_out, axis=-1), "head")
     inverse_rms = lax.rsqrt(square_sum / full_channels + EPSILON)
     normed_full = space_out * inverse_rms[:, None]
@@ -316,12 +356,12 @@
     ).astype(BF16)
     grad_query_space, grad_key_space, grad_value_space = call(
         space_backward_kernel,
-        [head_block()] * 4 + [mask_spec, mask_spec],
+        [head_block()] * 4 + [pl.BlockSpec((1, rows, rows), lambda h: (h, 0, 0))],
         [head_block()] * 3,
         [whole] * 3,
-        flops=6 * product,
-        traffic=7 * size,
-    )(q_space, k_space, v_space, grad_space_out, space_q_mask, space_k_mask)
+        flops=4 * product,
+        traffic=15 * size,
+    )(q_space, k_space, v_space, grad_space_out, *here_in(pltpu.HBM, space_weights))
 
     mixed, grad_query_time, grad_key_time = local(
         finish_kernel,

time: 123 us -> 118 us (0.959)
  blocking collectives: 50.5 us -> 48 us
  other arithmetic: 6.5 us -> 4.19 us
  Pallas kernels: 16.2 us -> 18.3 us
  waiting for transfers between devices: 13.3 us -> 11.7 us
    all_to_all x1, blocking collectives: 29.3 us -> 26.6 us  [exchange(): lax.all_to_all(blocks, 'frame', split_axis=0, concat_axis=0, tiled=True,...]
    pallas_call x3, Pallas kernels: 10.2 us -> 12.4 us  [the longest x1 7.06 us: per_device(): local(pack_kernel, [hbm] * 8, [hbm, vmem, hbm], [pltpu.HBM((rows, 3 * cha...]
    all_to_all x2, waiting for transfers between devices: 13.3 us -> 11.7 us  [exchange(): lax.all_to_all(blocks, 'frame', split_axis=0, concat_axis=0, tiled=True,...]
    convert_element_type x3 -> x0, other arithmetic: 1.33 us -> none  [the longest x1 0.68 us: per_device(): live_space[:, None].astype(F32)]
  transfers between devices with their start and end apart: 2 -> 2, of which waited for: 2 -> 2; matrix products, arithmetic and copies ran while one was open for 6% -> 4% of each run, Pallas kernels for 7% -> 5%
where the time goes in v5:
time: 118 us
  blocking collectives  48 us (41%)
  starting transfers between devices  32.9 us (28%)
  Pallas kernels  18.3 us (16%)
  waiting for transfers between devices  11.7 us (10%)
  other arithmetic  4.19 us (4%)
  between operations  1.68 us (1%)
    all_to_all x2, starting transfers between devices, exchange(): lax.all_to_all(blocks, 'frame', split_axis=0, concat_axis=0, tiled=True,...  32.9 us
    all_to_all x1, blocking collectives, exchange(): lax.all_to_all(blocks, 'frame', split_axis=0, concat_axis=0, tiled=True,...  26.6 us
    all_to_all x2, waiting for transfers between devices, exchange(): lax.all_to_all(blocks, 'frame', split_axis=0, concat_axis=0, tiled=True,...  11.7 us
    psum x1, blocking collectives, per_device(): inner_norm = lax.psum(jnp.sum(grad_norm * normed_full, axis=-1), 'head')  10.7 us
    psum x1, blocking collectives, per_device(): square_sum = lax.psum(jnp.sum(space_out * space_out, axis=-1), 'head')  10.6 us
    pallas_call x1, Pallas kernels, per_device(): local(pack_kernel, [hbm] * 8, [hbm, vmem, hbm], [pltpu.HBM((rows, 3 * cha...  7.06 us
    pallas_call x1, Pallas kernels, per_device(): call(space_backward_kernel, [head_block()] * 4 + [pl.BlockSpec((1, rows,...  5.2 us
    pallas_call x1, Pallas kernels, per_device(): local(time_rest_kernel, [vmem] * 5, hbm, pltpu.HBM((rows, 3 * channels),...  3.27 us
  transfers between devices with their start and end apart: 2, of which 2 were waited for; matrix products, arithmetic and copies ran while one was open for 4% of the time, Pallas kernels for 5%

profile of v5, /device:TPU:6, one launch (start us, length us, event | category | flops | bytes accessed | tf_op | source)
XLA Modules:
  0.0 117.6 jit_solution(11820048404337729209)
XLA Ops:
  0.6 7.1 %shard_map.127 = (bf16[512,1152]{1,0:T(8,128)(2,1)}, f32[512,384]{1,0:T(8,128)S(1)}, f32[3,512,512]{2,1,0:T(8,128)}) custom-call(bf16[512,384]{1,0:T(8,128)(2,1)} %bitcast.22, bf16[512,384]{1,0:T(8,128)(2,1)} %bitcast.25, bf16[512,384]{1,0:T(8,128)(2,1)} %bitcast.28, s32[64]{0:T(128)} %clip_ref.3, s32[6]{0:T(128)} %res_ref.3, bf16[512,384]{1,0:T(8,128)(2,1)} %bitcast.40, ...), custom_call_target="tpu_custom_call" | custom-call | bytes 2359296 | tf_op jit(solution)/shard_map/pallas_call | solution.py:290
  7.7 0.0 copy-start.5
  7.7 0.0 copy-start.6
  7.7 19.9 %all-to-all-start = ((bf16[64,8,1152]{2,1,0:T(8,128)(2,1)}), bf16[64,8,1152]{2,1,0:T(8,128)(2,1)S(1)}, u32[]{:S(2)}, u32[]{:S(2)}) async-start(bf16[64,8,1152]{2,1,0:T(8,128)(2,1)} %bitcast.38), calls=%async_computation | async-start | bytes 2359296 | tf_op jit(solution)/shard_map/all_to_all | solution.py:269
  27.6 0.0 copy-done.5
  27.6 0.0 copy-done.6
  27.6 0.1 select_reduce_fusion.2
  27.7 0.2 select_reduce_fusion
  27.9 0.1 iota_add_fusion
  28.0 0.1 add.244
  28.1 0.6 fusion.15
  29.4 0.1 fusion.16
  29.5 0.1 lt.74
  29.6 0.1 reshape.175.live_ref
  29.7 0.1 shard_map.128
  29.8 0.1 multiply_reduce_fusion.1
  29.9 10.6 %psum.14 = f32[512]{0:T(512)S(1)} all-reduce(f32[512]{0:T(512)S(1)} %multiply_reduce_fusion.1), channel_id=1, replica_groups=mesh['frame'=64,'head'=8] {'head'}, use_global_device_ids=true, to_apply=%region_1.2 | all-reduce | flops 512 | bytes 4096 | tf_op jit(solution)/shard_map/psum | solution.py:324
  40.5 0.1 fusion.1.q_mask_ref
  40.7 0.2 select_convert_fusion.k_mask_ref
  40.9 0.1 multiply_convert_fusion.1.normed_ref
  41.0 8.2 %all-to-all-done = bf16[64,8,1152]{2,1,0:T(8,128)(2,1)S(1)} async-done(((bf16[64,8,1152]{2,1,0:T(8,128)(2,1)}), bf16[64,8,1152]{2,1,0:T(8,128)(2,1)S(1)}, u32[]{:S(2)}, u32[]{:S(2)}) %all-to-all-start) | async-done | bytes 1179680 | tf_op jit(solution)/shard_map/all_to_all | solution.py:269
  49.2 1.6 %shard_map.129 = (bf16[512,768]{1,0:T(8,128)(2,1)S(1)}, f32[8,512]{1,0:T(8,128)S(1)}) custom-call(bf16[512,1152]{1,0:T(8,128)(2,1)S(1)} %bitcast.34, bf16[512,384]{1,0:T(8,128)(2,1)S(1)} %multiply_convert_fusion.1.normed_ref, bf16[512,128]{1,0:T(8,128)(2,1)S(1)} %fusion.1.q_mask_ref, bf16[512,128]{1,0:T(8,128)(2,1)S(1)} %select_convert_fusion.k_mask_ref, ...), custom_call_target="tpu_custom_call" | custom-call | flops 603979776 | bytes 2359296 | tf_op jit(solution)/shard_map/pallas_call | solution.py:329
  50.9 26.6 %all_to_all.15 = bf16[64,8,768]{2,1,0:T(8,128)(2,1)S(1)} all-to-all(bf16[64,8,768]{2,1,0:T(8,128)(2,1)S(1)} %bitcast.36), channel_id=1, replica_groups={{288,296,304,312,256,264,272,280,352,360,368,376,320,328,336,344,416,42..., dimensions={0} | all-to-all | bytes 1572864 | tf_op jit(solution)/shard_map/all_to_all | solution.py:269
  77.5 0.0 copy-start.3
  77.5 3.3 %shard_map.130 = bf16[512,1152]{1,0:T(8,128)(2,1)} custom-call(bf16[512,1152]{1,0:T(8,128)(2,1)S(1)} %bitcast.35, bf16[512,768]{1,0:T(8,128)(2,1)S(1)} %bitcast.31, bf16[512,128]{1,0:T(8,128)(2,1)S(1)} %fusion.1.q_mask_ref, bf16[512,128]{1,0:T(8,128)(2,1)S(1)} %select_convert_fusion.k_mask_ref, f32[8,512]{1,0:T(8,128)S(1)} %get-tuple-element.24.shift_ref), custom_call_target="tpu_custom_call" | custom-call | flops 1207959552 | bytes 3145728 | tf_op jit(solution)/shard_map/pallas_call | solution.py:339
  80.8 0.0 copy-start.4
  80.8 13.0 %all-to-all-start.2 = ((bf16[64,8,1152]{2,1,0:T(8,128)(2,1)}), bf16[64,8,1152]{2,1,0:T(8,128)(2,1)S(1)}, u32[]{:S(2)}, u32[]{:S(2)}) async-start(bf16[64,8,1152]{2,1,0:T(8,128)(2,1)} %bitcast.39), calls=%async_computation.2 | async-start | bytes 2359296 | tf_op jit(solution)/shard_map/all_to_all | solution.py:269
  93.8 0.6 dynamic_slice.3
  94.4 0.6 iota_compare_fusion.3
  95.0 0.0 copy-done.3
  95.0 0.0 copy-done.4
  95.1 0.4 multiply_reduce_fusion
  95.5 0.0 copy-start
  95.5 0.0 copy-start.1
  95.5 0.0 copy-start.2
  95.5 10.7 %psum.15 = f32[512]{0:T(512)S(1)} all-reduce(f32[512]{0:T(512)S(1)} %multiply_reduce_fusion), channel_id=1, replica_groups=mesh['frame'=64,'head'=8] {'head'}, use_global_device_ids=true, to_apply=%region_7.8 | all-reduce | flops 512 | bytes 4096 | tf_op jit(solution)/shard_map/psum | solution.py:353
  106.2 1.4 %multiply_convert_fusion.g_ref = bf16[512,384]{1,0:T(8,128)(2,1)S(1)} fusion(f32[512,384]{1,0:T(8,128)S(1)} %get-tuple-element.22, f32[512]{0:T(512)S(1)} %broadcast_multiply_fusion, f32[512]{0:T(512)S(1)} %add_rsqrt_fusion, bf16[512,768]{1,0:T(8,128)(2,1)} %bitcast.33, pred[512]{0:T(512)(128)(4,1)S(1)} %iota_compare_fusion.3, bf16[1,512,384]{2,1,0:T(8,128)(2,1)} %param.13), kind=kLoop, calls=%fused_computation | loop fusion | flops 1769472 | bytes 1970688 | tf_op jit(solution)/shard_map/convert_element_type | solution.py:356
  107.7 0.0 copy-done
  107.7 0.0 copy-done.1
  107.7 0.0 copy-done.2
  107.7 5.2 %shard_map.132 = (bf16[512,384]{1,0:T(8,128)(2,1)}, bf16[512,384]{1,0:T(8,128)(2,1)}, bf16[512,384]{1,0:T(8,128)(2,1)}) custom-call(bf16[512,384]{1,0:T(8,128)(2,1)S(1)} %bitcast.24, bf16[512,384]{1,0:T(8,128)(2,1)S(1)} %bitcast.27, bf16[512,384]{1,0:T(8,128)(2,1)S(1)} %bitcast.30, bf16[512,384]{1,0:T(8,128)(2,1)S(1)} %multiply_convert_fusion.g_ref, ...), custom_call_target="tpu_custom_call" | custom-call | flops 805306368 | bytes 5898240 | tf_op jit(solution)/shard_map/pallas_call | solution.py:357
  112.9 3.5 %all-to-all-done.2 = bf16[64,8,1152]{2,1,0:T(8,128)(2,1)S(1)} async-done(((bf16[64,8,1152]{2,1,0:T(8,128)(2,1)}), bf16[64,8,1152]{2,1,0:T(8,128)(2,1)S(1)}, u32[]{:S(2)}, u32[]{:S(2)}) %all-to-all-start.2) | async-done | bytes 1179680 | tf_op jit(solution)/shard_map/all_to_all | solution.py:269
  116.4 1.0 shard_map.131
  (5 shorter events, 0.0 us)
Async XLA Ops:
  7.7 19.9 %copy-start.5 = (s32[64]{0:T(128)S(1)}, s32[64]{0:T(128)}, u32[]{:S(2)}) copy-start(s32[64]{0:T(128)} %clip_ref.3) | copy-start | bytes 772
  7.7 19.9 %copy-start.6 = (s32[6]{0:T(128)S(1)}, s32[6]{0:T(128)}, u32[]{:S(2)}) copy-start(s32[6]{0:T(128)} %res_ref.3) | copy-start | bytes 76
  7.7 41.5 %all-to-all-start = ((bf16[64,8,1152]{2,1,0:T(8,128)(2,1)}), bf16[64,8,1152]{2,1,0:T(8,128)(2,1)S(1)}, u32[]{:S(2)}, u32[]{:S(2)}) async-start(bf16[64,8,1152]{2,1,0:T(8,128)(2,1)} %bitcast.38), calls=%async_computation | async-start | bytes 2359296 | tf_op jit(solution)/shard_map/all_to_all | solution.py:269
  77.5 17.5 %copy-start.3 = (bf16[64,8,768]{2,1,0:T(8,128)(2,1)}, bf16[64,8,768]{2,1,0:T(8,128)(2,1)S(1)}, u32[]{:S(2)}) copy-start(bf16[64,8,768]{2,1,0:T(8,128)(2,1)S(1)} %all_to_all.15) | copy-start | bytes 2359300
  80.8 14.3 %copy-start.4 = (bf16[1,512,384]{2,1,0:T(8,128)(2,1)S(1)}, bf16[1,512,384]{2,1,0:T(8,128)(2,1)}, u32[]{:S(2)}) copy-start(bf16[1,512,384]{2,1,0:T(8,128)(2,1)} %param.13) | copy-start | bytes 1179652
  80.8 35.6 %all-to-all-start.2 = ((bf16[64,8,1152]{2,1,0:T(8,128)(2,1)}), bf16[64,8,1152]{2,1,0:T(8,128)(2,1)S(1)}, u32[]{:S(2)}, u32[]{:S(2)}) async-start(bf16[64,8,1152]{2,1,0:T(8,128)(2,1)} %bitcast.39), calls=%async_computation.2 | async-start | bytes 2359296 | tf_op jit(solution)/shard_map/all_to_all | solution.py:269
  95.5 12.2 %copy-start = (bf16[1,512,384]{2,1,0:T(8,128)(2,1)S(1)}, bf16[1,512,384]{2,1,0:T(8,128)(2,1)}, u32[]{:S(2)}) copy-start(bf16[1,512,384]{2,1,0:T(8,128)(2,1)} %param.8) | copy-start | bytes 1179652
  95.5 12.2 %copy-start.1 = (bf16[1,512,384]{2,1,0:T(8,128)(2,1)S(1)}, bf16[1,512,384]{2,1,0:T(8,128)(2,1)}, u32[]{:S(2)}) copy-start(bf16[1,512,384]{2,1,0:T(8,128)(2,1)} %param.9) | copy-start | bytes 1179652
  95.5 12.2 %copy-start.2 = (bf16[1,512,384]{2,1,0:T(8,128)(2,1)S(1)}, bf16[1,512,384]{2,1,0:T(8,128)(2,1)}, u32[]{:S(2)}) copy-start(bf16[1,512,384]{2,1,0:T(8,128)(2,1)} %param.10) | copy-start | bytes 1179652

commit v6 on v5

--- a/solution.py
+++ b/solution.py
@@ -13,7 +13,7 @@
 BF16 = jnp.bfloat16
 VMEM_BYTES = 24 * 1024 * 1024
 LOWEST = -3e38
-Z_PLACES = (4, 5, 6, 7, 0, 1, 2, 3)
+Z_PLACES = (5, 6, 7, 0, 1, 2, 3, 4)
 Y_PLACES = (4, 5, 6, 7, 0, 1, 2, 3)
 
 
@@ -124,21 +124,30 @@
     width = normed_ref.shape[1]
     out_ref[:, :width] = normed_ref[...]
     q_mask, k_mask, live = q_mask_ref[...], k_mask_ref[...], live_ref[...]
-    for h in range(width // HD):
-        q, k, g = (
-            moved_ref[:, j * width + h * HD : j * width + (h + 1) * HD] for j in range(3)
-        )
-        scores = dot(
-            jnp.concatenate([k, k_mask], axis=1), jnp.concatenate([q, q_mask], axis=1), 1, 1
-        )
-        highest = jnp.max(scores, axis=0, keepdims=True)
-        expanded = jnp.exp2((scores - highest) * scale)
+    heads = range(width // HD)
+
+    def moved(j, h):
+        return moved_ref[:, j * width + h * HD : j * width + (h + 1) * HD]
+
+    scores = [
+        dot(
+            jnp.concatenate([moved(1, h), k_mask], axis=1),
+            jnp.concatenate([moved(0, h), q_mask], axis=1),
+            1,
+            1,
+        )
+        for h in heads
+    ]
+    for h in heads:
+        highest = jnp.max(scores[h], axis=0, keepdims=True)
+        expanded = jnp.exp2((scores[h] - highest) * scale)
         inverse = 1.0 / jnp.sum(expanded, axis=0, keepdims=True)
         weights = (expanded * (inverse * live)).astype(BF16)
         shift_ref[h : h + 1, :] = jnp.where(
             live > 0, jnp.log2(inverse) - highest * scale, LOWEST
         )
-        out_ref[:, width + h * HD : width + (h + 1) * HD] = dot(weights, g, 1, 0).astype(BF16)
+        grad_value = dot(weights, moved(2, h), 1, 0)
+        out_ref[:, width + h * HD : width + (h + 1) * HD] = grad_value.astype(BF16)
 
 
 def time_rest_kernel(

time: 118 us -> 115 us (0.975); the launches traced: 118 us -> 113 us
  blocking collectives: 48 us -> 46 us
  starting transfers between devices: 32.9 us -> 30.9 us
    all_to_all x1, blocking collectives: 26.6 us -> 24.6 us  [exchange(): lax.all_to_all(blocks, 'frame', split_axis=0, concat_axis=0, tiled=True,...]
    all_to_all x2, starting transfers between devices: 32.9 us -> 30.9 us  [exchange(): lax.all_to_all(blocks, 'frame', split_axis=0, concat_axis=0, tiled=True,...]
where the time goes in v6:
time: 115 us; the launch traced here: 113 us
  blocking collectives  46 us (40%)
  starting transfers between devices  30.9 us (27%)
  Pallas kernels  18.1 us (16%)
  waiting for transfers between devices  11 us (10%)
  other arithmetic  4.2 us (4%)
  between operations  1.68 us (1%)
    all_to_all x2, starting transfers between devices, exchange(): lax.all_to_all(blocks, 'frame', split_axis=0, concat_axis=0, tiled=True,...  30.9 us
    all_to_all x1, blocking collectives, exchange(): lax.all_to_all(blocks, 'frame', split_axis=0, concat_axis=0, tiled=True,...  24.6 us
    all_to_all x2, waiting for transfers between devices, exchange(): lax.all_to_all(blocks, 'frame', split_axis=0, concat_axis=0, tiled=True,...  11 us
    psum x1, blocking collectives, per_device(): inner_norm = lax.psum(jnp.sum(grad_norm * normed_full, axis=-1), 'head')  10.7 us
    psum x1, blocking collectives, per_device(): square_sum = lax.psum(jnp.sum(space_out * space_out, axis=-1), 'head')  10.6 us
    pallas_call x1, Pallas kernels, per_device(): local(pack_kernel, [hbm] * 8, [hbm, vmem, hbm], [pltpu.HBM((rows, 3 * cha...  7.06 us
    pallas_call x1, Pallas kernels, per_device(): call(space_backward_kernel, [head_block()] * 4 + [pl.BlockSpec((1, rows,...  5.2 us
    pallas_call x1, Pallas kernels, per_device(): local(time_rest_kernel, [vmem] * 5, hbm, pltpu.HBM((rows, 3 * channels),...  3.27 us
  transfers between devices with their start and end apart: 2, of which 2 were waited for; matrix products, arithmetic and copies ran while one was open for 4% of the time, Pallas kernels for 5%

profile of v6, /device:TPU:6, one launch (start us, length us, event | category | flops | bytes accessed | tf_op | source)
XLA Modules:
  0.0 112.9 jit_solution(5963216820692705423)
XLA Ops:
  0.6 7.1 %shard_map.127 = (bf16[512,1152]{1,0:T(8,128)(2,1)}, f32[512,384]{1,0:T(8,128)S(1)}, f32[3,512,512]{2,1,0:T(8,128)}) custom-call(bf16[512,384]{1,0:T(8,128)(2,1)} %bitcast.22, bf16[512,384]{1,0:T(8,128)(2,1)} %bitcast.25, bf16[512,384]{1,0:T(8,128)(2,1)} %bitcast.28, s32[64]{0:T(128)} %clip_ref.3, s32[6]{0:T(128)} %res_ref.3, bf16[512,384]{1,0:T(8,128)(2,1)} %bitcast.40, ...), custom_call_target="tpu_custom_call" | custom-call | bytes 2359296 | tf_op jit(solution)/shard_map/pallas_call | solution.py:299
  7.7 0.0 copy-start.5
  7.7 0.0 copy-start.6
  7.7 18.9 %all-to-all-start = ((bf16[64,8,1152]{2,1,0:T(8,128)(2,1)}), bf16[64,8,1152]{2,1,0:T(8,128)(2,1)S(1)}, u32[]{:S(2)}, u32[]{:S(2)}) async-start(bf16[64,8,1152]{2,1,0:T(8,128)(2,1)} %bitcast.38), calls=%async_computation | async-start | bytes 2359296 | tf_op jit(solution)/shard_map/all_to_all | solution.py:278
  26.7 0.0 copy-done.5
  26.7 0.0 copy-done.6
  26.7 0.1 select_reduce_fusion.2
  26.8 0.2 select_reduce_fusion
  27.0 0.1 iota_add_fusion
  27.0 0.1 add.244
  27.1 0.6 fusion.15
  28.4 0.1 fusion.16
  28.5 0.1 lt.74
  28.6 0.1 reshape.175.live_ref
  28.7 0.1 shard_map.128
  28.8 0.1 multiply_reduce_fusion.1
  29.0 10.6 %psum.14 = f32[512]{0:T(512)S(1)} all-reduce(f32[512]{0:T(512)S(1)} %multiply_reduce_fusion.1), channel_id=1, replica_groups=mesh['frame'=64,'head'=8] {'head'}, use_global_device_ids=true, to_apply=%region_1.2 | all-reduce | flops 512 | bytes 4096 | tf_op jit(solution)/shard_map/psum | solution.py:333
  39.6 0.1 fusion.1.q_mask_ref
  39.7 0.2 select_convert_fusion.k_mask_ref
  39.9 0.1 multiply_convert_fusion.1.normed_ref
  40.1 9.1 %all-to-all-done = bf16[64,8,1152]{2,1,0:T(8,128)(2,1)S(1)} async-done(((bf16[64,8,1152]{2,1,0:T(8,128)(2,1)}), bf16[64,8,1152]{2,1,0:T(8,128)(2,1)S(1)}, u32[]{:S(2)}, u32[]{:S(2)}) %all-to-all-start) | async-done | bytes 1179680 | tf_op jit(solution)/shard_map/all_to_all | solution.py:278
  49.2 1.5 %shard_map.129 = (bf16[512,768]{1,0:T(8,128)(2,1)S(1)}, f32[8,512]{1,0:T(8,128)S(1)}) custom-call(bf16[512,1152]{1,0:T(8,128)(2,1)S(1)} %bitcast.34, bf16[512,384]{1,0:T(8,128)(2,1)S(1)} %multiply_convert_fusion.1.normed_ref, bf16[512,128]{1,0:T(8,128)(2,1)S(1)} %fusion.1.q_mask_ref, bf16[512,128]{1,0:T(8,128)(2,1)S(1)} %select_convert_fusion.k_mask_ref, ...), custom_call_target="tpu_custom_call" | custom-call | flops 603979776 | bytes 2359296 | tf_op jit(solution)/shard_map/pallas_call | solution.py:338
  50.7 24.6 %all_to_all.15 = bf16[64,8,768]{2,1,0:T(8,128)(2,1)S(1)} all-to-all(bf16[64,8,768]{2,1,0:T(8,128)(2,1)S(1)} %bitcast.36), channel_id=1, replica_groups={{352,360,368,376,320,328,336,344,416,424,432,440,384,392,400,408,480,48..., dimensions={0} | all-to-all | bytes 1572864 | tf_op jit(solution)/shard_map/all_to_all | solution.py:278
  75.3 0.0 copy-start.3
  75.3 3.3 %shard_map.130 = bf16[512,1152]{1,0:T(8,128)(2,1)} custom-call(bf16[512,1152]{1,0:T(8,128)(2,1)S(1)} %bitcast.35, bf16[512,768]{1,0:T(8,128)(2,1)S(1)} %bitcast.31, bf16[512,128]{1,0:T(8,128)(2,1)S(1)} %fusion.1.q_mask_ref, bf16[512,128]{1,0:T(8,128)(2,1)S(1)} %select_convert_fusion.k_mask_ref, f32[8,512]{1,0:T(8,128)S(1)} %get-tuple-element.24.shift_ref), custom_call_target="tpu_custom_call" | custom-call | flops 1207959552 | bytes 3145728 | tf_op jit(solution)/shard_map/pallas_call | solution.py:348
  78.6 0.0 copy-start.4
  78.6 12.0 %all-to-all-start.2 = ((bf16[64,8,1152]{2,1,0:T(8,128)(2,1)}), bf16[64,8,1152]{2,1,0:T(8,128)(2,1)S(1)}, u32[]{:S(2)}, u32[]{:S(2)}) async-start(bf16[64,8,1152]{2,1,0:T(8,128)(2,1)} %bitcast.39), calls=%async_computation.2 | async-start | bytes 2359296 | tf_op jit(solution)/shard_map/all_to_all | solution.py:278
  90.6 0.6 dynamic_slice.3
  91.2 0.6 iota_compare_fusion.3
  91.9 0.0 copy-done.3
  91.9 0.0 copy-done.4
  91.9 0.4 multiply_reduce_fusion
  92.3 0.0 copy-start
  92.3 0.0 copy-start.1
  92.3 0.0 copy-start.2
  92.4 10.7 %psum.15 = f32[512]{0:T(512)S(1)} all-reduce(f32[512]{0:T(512)S(1)} %multiply_reduce_fusion), channel_id=1, replica_groups=mesh['frame'=64,'head'=8] {'head'}, use_global_device_ids=true, to_apply=%region_7.8 | all-reduce | flops 512 | bytes 4096 | tf_op jit(solution)/shard_map/psum | solution.py:362
  103.1 1.4 %multiply_convert_fusion.g_ref = bf16[512,384]{1,0:T(8,128)(2,1)S(1)} fusion(f32[512,384]{1,0:T(8,128)S(1)} %get-tuple-element.22, f32[512]{0:T(512)S(1)} %broadcast_multiply_fusion, f32[512]{0:T(512)S(1)} %add_rsqrt_fusion, bf16[512,768]{1,0:T(8,128)(2,1)} %bitcast.33, pred[512]{0:T(512)(128)(4,1)S(1)} %iota_compare_fusion.3, bf16[1,512,384]{2,1,0:T(8,128)(2,1)} %param.13), kind=kLoop, calls=%fused_computation | loop fusion | flops 1769472 | bytes 1970688 | tf_op jit(solution)/shard_map/convert_element_type | solution.py:365
  104.5 0.0 copy-done
  104.5 0.0 copy-done.1
  104.6 0.0 copy-done.2
  104.6 5.2 %shard_map.132 = (bf16[512,384]{1,0:T(8,128)(2,1)}, bf16[512,384]{1,0:T(8,128)(2,1)}, bf16[512,384]{1,0:T(8,128)(2,1)}) custom-call(bf16[512,384]{1,0:T(8,128)(2,1)S(1)} %bitcast.24, bf16[512,384]{1,0:T(8,128)(2,1)S(1)} %bitcast.27, bf16[512,384]{1,0:T(8,128)(2,1)S(1)} %bitcast.30, bf16[512,384]{1,0:T(8,128)(2,1)S(1)} %multiply_convert_fusion.g_ref, ...), custom_call_target="tpu_custom_call" | custom-call | flops 805306368 | bytes 5898240 | tf_op jit(solution)/shard_map/pallas_call | solution.py:366
  109.8 1.9 %all-to-all-done.2 = bf16[64,8,1152]{2,1,0:T(8,128)(2,1)S(1)} async-done(((bf16[64,8,1152]{2,1,0:T(8,128)(2,1)}), bf16[64,8,1152]{2,1,0:T(8,128)(2,1)S(1)}, u32[]{:S(2)}, u32[]{:S(2)}) %all-to-all-start.2) | async-done | bytes 1179680 | tf_op jit(solution)/shard_map/all_to_all | solution.py:278
  111.7 1.0 shard_map.131
  (5 shorter events, 0.0 us)
Async XLA Ops:
  7.7 19.0 %copy-start.5 = (s32[64]{0:T(128)S(1)}, s32[64]{0:T(128)}, u32[]{:S(2)}) copy-start(s32[64]{0:T(128)} %clip_ref.3) | copy-start | bytes 772
  7.7 19.0 %copy-start.6 = (s32[6]{0:T(128)S(1)}, s32[6]{0:T(128)}, u32[]{:S(2)}) copy-start(s32[6]{0:T(128)} %res_ref.3) | copy-start | bytes 76
  7.7 41.5 %all-to-all-start = ((bf16[64,8,1152]{2,1,0:T(8,128)(2,1)}), bf16[64,8,1152]{2,1,0:T(8,128)(2,1)S(1)}, u32[]{:S(2)}, u32[]{:S(2)}) async-start(bf16[64,8,1152]{2,1,0:T(8,128)(2,1)} %bitcast.38), calls=%async_computation | async-start | bytes 2359296 | tf_op jit(solution)/shard_map/all_to_all | solution.py:278
  75.3 16.6 %copy-start.3 = (bf16[64,8,768]{2,1,0:T(8,128)(2,1)}, bf16[64,8,768]{2,1,0:T(8,128)(2,1)S(1)}, u32[]{:S(2)}) copy-start(bf16[64,8,768]{2,1,0:T(8,128)(2,1)S(1)} %all_to_all.15) | copy-start | bytes 2359300
  78.6 13.3 %copy-start.4 = (bf16[1,512,384]{2,1,0:T(8,128)(2,1)S(1)}, bf16[1,512,384]{2,1,0:T(8,128)(2,1)}, u32[]{:S(2)}) copy-start(bf16[1,512,384]{2,1,0:T(8,128)(2,1)} %param.13) | copy-start | bytes 1179652
  78.6 33.1 %all-to-all-start.2 = ((bf16[64,8,1152]{2,1,0:T(8,128)(2,1)}), bf16[64,8,1152]{2,1,0:T(8,128)(2,1)S(1)}, u32[]{:S(2)}, u32[]{:S(2)}) async-start(bf16[64,8,1152]{2,1,0:T(8,128)(2,1)} %bitcast.39), calls=%async_computation.2 | async-start | bytes 2359296 | tf_op jit(solution)/shard_map/all_to_all | solution.py:278
  92.3 12.2 %copy-start = (bf16[1,512,384]{2,1,0:T(8,128)(2,1)S(1)}, bf16[1,512,384]{2,1,0:T(8,128)(2,1)}, u32[]{:S(2)}) copy-start(bf16[1,512,384]{2,1,0:T(8,128)(2,1)} %param.8) | copy-start | bytes 1179652
  92.3 12.2 %copy-start.1 = (bf16[1,512,384]{2,1,0:T(8,128)(2,1)S(1)}, bf16[1,512,384]{2,1,0:T(8,128)(2,1)}, u32[]{:S(2)}) copy-start(bf16[1,512,384]{2,1,0:T(8,128)(2,1)} %param.9) | copy-start | bytes 1179652
  92.3 12.2 %copy-start.2 = (bf16[1,512,384]{2,1,0:T(8,128)(2,1)S(1)}, bf16[1,512,384]{2,1,0:T(8,128)(2,1)}, u32[]{:S(2)}) copy-start(bf16[1,512,384]{2,1,0:T(8,128)(2,1)} %param.10) | copy-start | bytes 1179652
